TPU v7x, 32 devices: a whole 2x2x4 slice. The times are simulated.
32 devices in a mesh: prow: 8 (over z, y), pcol: 4 (over x, core).
Axes of the slice: x: 2, y: 2, z: 4, core: 2. Of those that a mesh axis runs over, the one named last changes fastest.
Arguments:
- matrix: bfloat16 [14336, 7168], P('prow', 'pcol'), may hold values from -6 to 6
- pivots: int32 [256], replicated, may hold values from 0 to 14335
Outputs:
- factored: bfloat16 [14336, 7168], P('prow', 'pcol')
All inputs are finite; a program needn't handle non-finite values.
Results may differ from a plain program's by a relative error of at most 0.0044.
Values may be sent and summed in bfloat16 or wider, within the bound.
No kernel may reach another device: no remote copies, remote signals or barrier semaphores. Data moves between devices by JAX's collectives and lax.ppermute only.
A program may use at most 64 MiB of HBM per device.

v0:
```python
import jax
import jax.numpy as jnp
from jax import lax
from jax.sharding import PartitionSpec as P

NB = 256


def broadcast(block, axis, owner):
    block = jnp.where(lax.axis_index(axis) == owner, block, jnp.zeros_like(block))
    return lax.psum(block, axis)


def storage_row(global_row, rows_local, row_groups):
    block_index = global_row // NB
    return block_index % row_groups * rows_local + block_index // row_groups * NB + global_row % NB


def latest_match(targets, pivots, bound):
    steps = jnp.arange(NB, dtype=jnp.int32)
    hits = (pivots[None, :] == targets[:, None]) & (steps[None, :] < bound[:, None])
    return jnp.max(jnp.where(hits, steps[None, :], -1), axis=1)


def swap_anchor(pivots, wanted_rows):
    steps = jnp.arange(NB, dtype=jnp.int32)
    before = latest_match(steps, pivots, steps)
    pointer = jnp.where(before >= 0, before, steps)
    for level in range(NB.bit_length()):
        pointer = pointer[pointer]
    earlier = latest_match(pivots, pivots, steps)
    top_anchor = jnp.where(earlier >= 0, pointer[jnp.clip(earlier, 0, NB - 1)], pivots)
    last_hit = latest_match(wanted_rows, pivots, jnp.full(wanted_rows.shape, NB, jnp.int32))
    lower_anchor = jnp.where(last_hit >= 0, pointer[jnp.clip(last_hit, 0, NB - 1)], wanted_rows)
    in_top = wanted_rows < NB
    wanted_anchor = jnp.where(in_top, top_anchor[jnp.clip(wanted_rows, 0, NB - 1)], lower_anchor)
    return (top_anchor, wanted_anchor)


def local(matrix, pivots):
    rows_local, cols_local = matrix.shape
    row_groups = lax.axis_size("prow")
    prow_index = lax.axis_index("prow")
    pcol_index = lax.axis_index("pcol")
    local_rows = jnp.arange(rows_local, dtype=jnp.int32)
    global_rows = (local_rows // NB * row_groups + prow_index) * NB + local_rows % NB
    top_anchor, sources = swap_anchor(pivots, global_rows)
    top_sources = storage_row(top_anchor, rows_local, row_groups)
    owners = top_sources // rows_local
    nothing = jnp.zeros((), jnp.bfloat16)
    picked = jnp.where((owners == prow_index)[:, None], matrix[top_sources % rows_local], nothing)
    new_top = lax.psum(picked.astype(jnp.float32).astype(jnp.bfloat16), "prow")
    old_top = broadcast(matrix[:NB], "prow", 0)
    is_moved = (sources != global_rows) & (global_rows >= NB)
    displaced = old_top[jnp.clip(sources, 0, NB - 1)]
    exchanged = jnp.where(is_moved[:, None], displaced, matrix)
    panel = broadcast(matrix[:, :NB], "pcol", 0)
    diagonal_block = broadcast(panel[:NB], "prow", 0)
    unit_lower = jnp.tril(diagonal_block.astype(jnp.float32), -1) + jnp.eye(NB, dtype=jnp.float32)
    upper_rows = lax.linalg.triangular_solve(
        unit_lower, new_top.astype(jnp.float32), left_side=True, lower=True, unit_diagonal=True
    ).astype(jnp.bfloat16)
    is_top = global_rows < NB
    multipliers = jnp.where(is_top[:, None], nothing, panel)
    product = jnp.dot(multipliers, upper_rows, preferred_element_type=jnp.float32)
    updated = (exchanged.astype(jnp.float32) - product).astype(jnp.bfloat16)
    with_top = jnp.concatenate([upper_rows, updated[NB:]], 0)
    result = jnp.where(is_top[:, None], with_top, updated)
    panel_column = (pcol_index == 0) & (jnp.arange(cols_local) < NB)
    return jnp.where(panel_column[None, :], matrix, result)


def solution(mesh):
    placed = (P("prow", "pcol"), P())
    return jax.shard_map(
        local, mesh=mesh, in_specs=placed, out_specs=P("prow", "pcol"), check_vma=False
    )
```

profile of v0, /device:TPU:6, one launch (start us, length us, event | category | flops | bytes accessed | tf_op | source)
XLA Modules:
  0.0 211.2 jit_solution(16349818268524829927)
XLA Ops:
  6.5 0.0 all-reduce.4.cloned.1.call-start
  6.5 0.0 copy-start.2
  6.5 2.2 %slice_select_fusion.1 = bf16[1792,256]{1,0:T(8,128)(2,1)} fusion(bf16[1792,1792]{1,0:T(8,128)(2,1)} %param.2, pred[]{:T(512)S(6)} %eq.30), kind=kLoop, calls=%fused_computation.27 | loop fusion | flops 458752 | bytes 1835009 | tf_op jit(solution)/shard_map/jit(_where)/select_n | solution.py:10
  8.8 0.0 all-reduce.4.cloned.1.call-update
  8.8 0.0 all-reduce.6.cloned.1.call-start
  8.8 1.0 select_reduce_fusion.2
  9.9 1.9 gather_fusion
  11.9 1.9 gather_fusion.1
  13.9 1.9 gather_fusion.2
  15.8 1.9 gather_fusion.3
  17.8 1.9 gather_fusion.4
  19.8 1.9 gather_fusion.5
  21.8 1.9 gather_fusion.6
  23.7 1.9 gather_fusion.7
  25.7 1.9 gather_fusion.8
  27.7 1.9 gather_fusion.9
  29.6 0.0 copy-done.2
  29.7 5.8 %gather_fusion.10 = bf16[256,1792]{1,0:T(8,128)(2,1)S(1)} fusion(bf16[1792,1792]{1,0:T(8,128)(2,1)} %param.2, s32[1024]{0:T(1024)S(1)} %pad_clamp_fusion.3), kind=kCustom, calls=%fused_computation.10 | custom fusion | bytes 1836032 | tf_op jit(solution)/shard_map/gather | solution.py:51
  35.5 2.6 %slice_select_fusion = (bf16[256,1792]{1,0:T(8,128)(2,1)}, bf16[256,1792]{1,0:T(8,128)(2,1)}) fusion(bf16[1792,1792]{1,0:T(8,128)(2,1)} %param.2, pred[]{:T(512)S(6)} %eq.31, bf16[256,1792]{1,0:T(8,128)(2,1)S(1)} %gather_fusion.10, pred[256]{0:T(512)(128)(4,1)S(1)} %get-tuple-element.28), kind=kLoop, calls=%fused_computation.26 | loop fusion | flops 917504 | bytes 3670273 | tf_op jit(solution)/shard_map/jit(_where)/select_n | solution.py:10
  38.1 7.5 %all-reduce.4.cloned.1.call-done = bf16[1792,256]{1,0:T(8,128)(2,1)} async-done(((bf16[1792,256]{1,0:T(8,128)(2,1)}), bf16[1792,256]{1,0:T(8,128)(2,1)}) %all-reduce.4.cloned.1.call-update) | async-done | bytes 917520 | tf_op jit(solution)/shard_map/psum | solution.py:11
  45.6 1.6 slice_select_fusion.2
  47.2 0.0 all-reduce.6.cloned.1.call-update
  47.2 0.7 select_reduce_fusion
  48.0 10.9 %gather_fusion.12 = s32[1792]{0:T(1024)S(1)} fusion(s32[256]{0:T(256)S(1)} %gather_fusion.8, s32[2048]{0:T(1024)S(1)} %pad_clamp_fusion.1), kind=kCustom, calls=%fused_computation.12 | custom fusion | bytes 21504 | tf_op jit(solution)/shard_map/gather | solution.py:34
  58.9 0.1 fusion.26
  59.0 10.9 %gather_fusion.11 = s32[1792]{0:T(1024)S(1)} fusion(s32[256]{0:T(256)S(1)} %get-tuple-element.30, s32[2048]{0:T(1024)S(1)} %pad_clamp_fusion.2), kind=kCustom, calls=%fused_computation.11 | custom fusion | bytes 21504 | tf_op jit(solution)/shard_map/gather | solution.py:36
  69.9 0.1 fusion.28
  70.0 79.4 %all-reduce.6.cloned.1.call-done = (bf16[256,1792]{1,0:T(8,128)(2,1)}, bf16[256,1792]{1,0:T(8,128)(2,1)}, bf16[256,256]{1,0:T(8,128)(2,1)}) async-done(((bf16[256,1792]{1,0:T(8,128)(2,1)}, bf16[256,1792]{1,0:T(8,128)(2,1)}, bf16[256,256]{1,0:T(8,128)(2,1)}), (bf16[256,1792]{1,0:T(8,128)(2,1)}, bf16[256,1792]{1,0:T(8,128)(2,1)}, bf16[256,256]{1,0:T(8,128)(2,1)})) %all-reduce.6.cloned.1.call-update) | async-done | bytes 1966096 | tf_op jit(solution)/shard_map/psum | solution.py:11
  149.4 0.0 copy-start
  149.4 1.1 convert_add_fusion
  150.5 0.1 triangular_solve.90
  150.6 4.0 %while.1 = (s32[]{:T(128)}, f32[256,256]{1,0:T(8,128)S(1)}, s32[2,2]{1,0:T(2,128)S(1)}, f32[2,128,128]{2,1,0:T(8,128)S(1)}, s32[]{:T(128)}) while((s32[]{:T(128)}, f32[256,256]{1,0:T(8,128)S(1)}, s32[2,2]{1,0:T(2,128)S(1)}, f32[2,128,128]{2,1,0:T(8,128)S(1)}, s32[]{:T(128)}) %tuple.26), condition=%wide.while_cond, body=%wide.while_body.sunk | while | flops 2 | bytes 131189 | solution.py:60
  150.6 0.6 fusion.45
  151.2 1.4 bitcast_dynamic-update-slice_fusion.2
  152.6 0.6 fusion.45
  153.2 1.4 bitcast_dynamic-update-slice_fusion.2
  154.6 19.9 %custom-call.3 = f32[2,128,128]{1,2,0:T(8,128)S(1)} custom-call(f32[2,128,128]{2,1,0:T(8,128)S(1)} %get-tuple-element.12), custom_call_target="InvertDiagBlocksLowerTriangular" | custom-call | tf_op jit(solution)/shard_map/triangular_solve | solution.py:60
  174.5 1.6 fusion.41
  176.1 1.9 convolution_subtract_fusion
  178.0 0.9 convolution_convert_fusion
  179.0 0.0 copy-done
  179.0 0.0 copy-start.1
  179.0 7.6 %gather_fusion.13 = bf16[1792,1792]{1,0:T(8,128)(2,1)} fusion(bf16[256,1792]{1,0:T(8,128)(2,1)S(1)} %copy-done, s32[2048]{0:T(1024)S(1)} %pad_clamp_fusion), kind=kCustom, calls=%fused_computation.13 | custom fusion | bytes 12852224 | tf_op jit(solution)/shard_map/gather | solution.py:55
  186.5 0.0 copy-done.1
  186.5 6.5 %subtract_convert_fusion = bf16[1792,1792]{1,0:T(8,128)(2,1)S(1)} fusion(bf16[1792,1792]{1,0:T(8,128)(2,1)} %gather_fusion.13, bf16[1792,1792]{1,0:T(8,128)(2,1)} %param.2, pred[1792]{0:T(1024)(128)(4,1)S(1)} %get-tuple-element.26, bf16[128,1792]{1,0:T(8,128)(2,1)S(1)} %convolution_convert_fusion, bf16[128,1792]{1,0:T(8,128)(2,1)S(1)} %get-tuple-element.33, ...), kind=kOutput, calls=%fused_computation.16 | convolution fusion | flops 1659305984 | bytes 21106176 | tf_op jit(solution)/shard_map/dot_general | solution.py:65
  193.0 0.4 slice.67
  193.4 11.0 %fusion = bf16[1792,1792]{1,0:T(8,128)(2,1)} fusion(bf16[1792,1792]{1,0:T(8,128)(2,1)} %param.2, bf16[1792,1792]{1,0:T(8,128)(2,1)S(1)} %subtract_convert_fusion, bf16[1536,1792]{1,0:T(8,128)(2,1)S(1)} %slice.67, bf16[128,1792]{1,0:T(8,128)(2,1)S(1)} %convolution_convert_fusion, bf16[128,1792]{1,0:T(8,128)(2,1)S(1)} %get-tuple-element.33, ...), kind=kLoop, calls=%fused_computation.18 | loop fusion | flops 25690112 | bytes 25693696 | tf_op jit(solution)/shard_map/jit(_where)/select_n | solution.py:70
  (39 shorter events, 0.3 us)
Async XLA Ops:
  6.5 39.1 %all-reduce.4.cloned.1.call-start = ((), (), s32[]{:S(2)}) async-start(), calls=%async_computation | async-start | bytes 1835008 | tf_op jit(solution)/shard_map/psum | solution.py:11
  6.5 23.1 %copy-start.2 = (s32[256]{0:T(256)S(1)}, s32[256]{0:T(256)}, u32[]{:S(2)}) copy-start(s32[256]{0:T(256)} %param.3) | copy-start | bytes 3076
  8.8 140.6 %all-reduce.6.cloned.1.call-start = ((), (), s32[]{:S(2)}) async-start(), calls=%async_computation.1 | async-start | bytes 3932160 | tf_op jit(solution)/shard_map/psum | solution.py:11
  149.4 29.6 %copy-start = (bf16[256,1792]{1,0:T(8,128)(2,1)S(1)}, bf16[256,1792]{1,0:T(8,128)(2,1)}, u32[]{:S(2)}) copy-start(bf16[256,1792]{1,0:T(8,128)(2,1)} %get-tuple-element.23) | copy-start | bytes 2752516
  179.0 7.6 %copy-start.1 = (bf16[1792,256]{1,0:T(8,128)(2,1)S(1)}, bf16[1792,256]{1,0:T(8,128)(2,1)}, u32[]{:S(2)}) copy-start(bf16[1792,256]{1,0:T(8,128)(2,1)} %all-reduce.4.cloned.1.call-done) | copy-start | bytes 2752516
Sparse Core Ops, SparseCore 0:
  9.7 35.8 all-reduce.3
  49.4 99.9 all-reduce.5
where the time goes:
time: 213 us; the launch traced here: 211 us
  waiting for transfers between devices  86.9 us (41%)
  local copies, waits for them, and re-layouts  59.1 us (28%)
  other arithmetic  40.4 us (19%)
  between operations  13.9 us (7%)
  matrix products  10.9 us (5%)
    psum x2, waiting for transfers between devices, broadcast(): return lax.psum(block, axis)  86.8 us
    another operation x4, other arithmetic, local(): lax.linalg.triangular_solve(unit_lower, new_top.astype(jnp.float32), left...  21 us
    gather x9, local copies, waits for them, and re-layouts, swap_anchor(): pointer = pointer[pointer]  17.5 us
    select_n x1, other arithmetic, local(): return jnp.where(panel_column[None, :], matrix, result)  11 us
    gather x1, local copies, waits for them, and re-layouts, swap_anchor(): pointer[jnp.clip(last_hit, 0, NB - 1)]  10.9 us
    gather x1, local copies, waits for them, and re-layouts, swap_anchor(): top_anchor[jnp.clip(wanted_rows, 0, NB - 1)]  10.9 us
    gather x1, local copies, waits for them, and re-layouts, local(): displaced = old_top[jnp.clip(sources, 0, NB - 1)]  7.55 us
    dot_general x1, matrix products, local(): jnp.dot(multipliers, upper_rows, preferred_element_type=jnp.float32)  6.49 us
  transfers between devices with their start and end apart: 2, of which 2 were waited for; matrix products, arithmetic and copies ran while one was open for 25% of the time, Pallas kernels for 0%

commit v1 on v0

--- a/solution.py
+++ b/solution.py
@@ -1,9 +1,310 @@
+import functools
+
 import jax
 import jax.numpy as jnp
 from jax import lax
+from jax.experimental import pallas as pl
+from jax.experimental.pallas import tpu as pltpu
 from jax.sharding import PartitionSpec as P
 
 NB = 256
+HALF = 128
+BF16 = jnp.bfloat16
+F32 = jnp.float32
+I32 = jnp.int32
+
+
+def grid_of(row_groups):
+    outer = 4 if row_groups % 4 == 0 else row_groups
+    return outer, row_groups // outer
+
+
+def round_rows(row_groups):
+    share = -(-3 * NB // (2 * row_groups))
+    return min(NB, -(-share // 16) * 16)
+
+
+def iota(shape, dim):
+    return lax.broadcasted_iota(I32, shape, dim)
+
+
+def dot(a, b, precision=None):
+    return jnp.dot(a, b, preferred_element_type=F32, precision=precision)
+
+
+def block_owner(global_row, row_groups):
+    block = lax.shift_right_logical(global_row, 8)
+    if row_groups & (row_groups - 1) == 0:
+        return block & (row_groups - 1), lax.shift_right_logical(block, row_groups.bit_length() - 1)
+    return lax.rem(block, row_groups), lax.div(block, row_groups)
+
+
+def plan_kernel(pivots, source, landing, anchor):
+    def start(k, _):
+        anchor[pivots[k]] = pivots[k]
+        return 0
+
+    def identity(k, _):
+        anchor[k] = k
+        return 0
+
+    def swap(k, _):
+        target = pivots[k]
+        at_column, at_target = anchor[k], anchor[target]
+        anchor[k] = at_target
+        anchor[target] = at_column
+        return 0
+
+    def write(k, _):
+        row = anchor[k]
+        source[0, k] = row
+        landing[0, k] = jnp.where(row >= NB, anchor[row], -1)
+        return 0
+
+    lax.fori_loop(0, NB, start, 0, unroll=8)
+    lax.fori_loop(0, NB, identity, 0, unroll=8)
+    lax.fori_loop(0, NB, swap, 0, unroll=8)
+    lax.fori_loop(0, NB, write, 0, unroll=8)
+
+
+def as_column(row):
+    n = row.shape[1]
+    wide = jnp.broadcast_to(row, (n, n))
+    on_diagonal = iota((n, n), 0) == iota((n, n), 1)
+    return jnp.sum(jnp.where(on_diagonal, wide, 0), axis=1, keepdims=True)
+
+
+def pick_kernel(row_groups, cap, source, landing, matrix, rows, gather, place, flag, *gives):
+    me = lax.axis_index("prow")
+    outer, inner = grid_of(row_groups)
+    src, land = source[...], landing[...]
+    owner, block = block_owner(src, row_groups)
+    local = block * NB + (src & (NB - 1))
+    is_owner = (iota((row_groups, NB), 0) == owner).astype(BF16)
+    upto = (iota((NB, NB), 0) <= iota((NB, NB), 1)).astype(BF16)
+    ranks = dot(is_owner, upto)
+    slot = jnp.sum(jnp.where(is_owner > 0, ranks, 0.0), axis=0, keepdims=True).astype(I32) - 1
+    flag[...] = jnp.broadcast_to(jnp.max(ranks, axis=(0, 1), keepdims=True).astype(I32), flag.shape)
+    code = jnp.where(slot < cap, owner * cap + slot, -1)
+
+    def table(first, count, values):
+        hit = code == iota((count, NB), 0) + first
+        return jnp.max(jnp.where(hit, values, -1), axis=1, keepdims=True)
+
+    my_rows = table(me * cap, cap, local)
+    chosen = (my_rows == iota((cap, matrix.shape[0]), 1)).astype(BF16)
+    rows[...] = dot(chosen, matrix[...]).astype(BF16)
+    old_top = matrix[:NB]
+    for j in range(inner):
+        wanted = jnp.concatenate([table((z * inner + j) * cap, cap, land) for z in range(outer)], 0)
+        chosen_top = (wanted == iota((outer * cap, NB), 1)).astype(BF16)
+        gives[j][...] = dot(chosen_top, old_top).astype(BF16)
+    code_column = as_column(code)
+    lands_column = as_column(jnp.where(land >= 0, local, -1))
+    mine = code_column - me * cap == iota((NB, HALF), 1)
+    mine = mine & (iota((NB, HALF), 1) < cap)
+    place[...] = jnp.max(jnp.where(mine, lands_column, -1), axis=0, keepdims=True)
+    my_outer, my_inner = me // inner, me % inner
+    for turn in range(inner):
+        for step in range(outer):
+            from_outer = lax.rem(my_outer - step + outer, outer)
+            from_inner = lax.rem(my_inner - turn + inner, inner)
+            first = (from_outer * inner + from_inner) * cap
+            at = (turn * outer + step) * cap
+            gather[:, at : at + cap] = (code_column == iota((NB, cap), 1) + first).astype(BF16)
+
+
+def pieces(x):
+    high = x.astype(BF16)
+    rest = x - high.astype(F32)
+    middle = rest.astype(BF16)
+    return high, middle, (rest - middle.astype(F32)).astype(BF16)
+
+
+def invert_kernel(block, inverse):
+    rows, cols = iota((NB, NB), 0), iota((NB, NB), 1)
+    lower = block[...].astype(F32)
+
+    def corner(size):
+        same = lax.div(rows, 2 * size) == lax.div(cols, 2 * size)
+        low_left = ((rows & size) > 0) & ((cols & size) == 0)
+        return jnp.where(same & low_left, lower, 0.0)
+
+    x = jnp.where(rows == cols, 1.0, 0.0) - corner(1)
+    size = 2
+    while size < HALF:
+        x = x - dot(x, dot(corner(size), x, lax.Precision.HIGHEST), lax.Precision.HIGHEST)
+        size *= 2
+    inverse[:HALF] = x[:HALF, :HALF]
+    inverse[HALF:] = x[HALF:, HALF:]
+
+
+def finish_kernel(row_groups, cap, *refs):
+    outer, _ = grid_of(row_groups)
+    matrix, block, inverse, panel, gather, place = refs[:6]
+    parts = refs[6 : 6 + row_groups]
+    arrived = refs[6 + row_groups : 6 + row_groups + outer]
+    out, left, keep, first, corner, second = refs[6 + row_groups + outer :]
+    tile = pl.program_id(0)
+    row_me, col_me = lax.axis_index("prow"), lax.axis_index("pcol")
+    height = matrix.shape[0]
+
+    @pl.when(tile == 0)
+    def _():
+        hit = iota((height, HALF), 0) == place[...]
+        kept = jnp.max(jnp.where(hit, 1.0, 0.0), axis=1, keepdims=True) == 0.0
+        keep[...] = jnp.where(jnp.broadcast_to(kept, keep.shape), 1.0, 0.0)
+        left[:, :NB] = -panel[...]
+        left[:, NB:] = hit[:, :cap].astype(BF16)
+        x1 = pieces(inverse[:HALF])
+        x2 = pieces(inverse[HALF:])
+        first[...] = jnp.concatenate(x1, 1)
+        second[...] = jnp.concatenate([x2[0], x2[0], x2[1], x2[1], x2[0], x2[2]], 1)
+        edge = block[HALF:, :HALF]
+        corner[...] = jnp.concatenate([edge, edge, edge], 1)
+
+        @pl.when(row_me == 0)
+        def _():
+            keep[:NB] = jnp.zeros((NB, HALF), F32)
+            left[:NB, :NB] = (iota((NB, NB), 0) == iota((NB, NB), 1)).astype(BF16)
+            left[:NB, NB:] = jnp.zeros((NB, cap), BF16)
+
+    is_panel = (tile == 0) & (col_me == 0)
+
+    @pl.when(is_panel)
+    def _():
+        out[...] = matrix[...]
+
+    @pl.when(jnp.logical_not(is_panel))
+    def _():
+        rows = jnp.concatenate([part[...] for part in parts], 0)
+        top = dot(gather[...], rows)
+        top1 = top[:HALF].astype(BF16)
+        upper1 = dot(first[...], jnp.concatenate([top1] * 3, 0))
+        rest = top[HALF:] - dot(corner[...], jnp.concatenate(pieces(upper1), 0))
+        high, middle, low = pieces(rest)
+        upper2 = dot(second[...], jnp.concatenate([high, middle, high, middle, low, high], 0))
+        swaps = jnp.where(row_me < row_groups // outer, arrived[0][...], jnp.zeros_like(arrived[0]))
+        for other in arrived[1:]:
+            swaps = swaps + other[...]
+        right = jnp.concatenate([upper1.astype(BF16), upper2.astype(BF16), swaps], 0)
+        change = dot(left[...], right)
+        kept = jnp.concatenate([keep[...], keep[...]], 1) > 0.0
+        out[...] = (jnp.where(kept, matrix[...].astype(F32), 0.0) + change).astype(BF16)
+
+
+def spread(value, axes, index, pairs_of_levels):
+    for pairs in pairs_of_levels:
+        received = lax.ppermute(value, axes, pairs)
+        takers = jnp.asarray([to for _, to in pairs], I32)
+        value = jnp.where(jnp.any(index == takers), received, value)
+    return value
+
+
+def tree(count, stride=1):
+    step, levels = count // 2, []
+    while step:
+        levels.append([(i * stride, (i + step) * stride) for i in range(0, count, 2 * step)])
+        step //= 2
+    return levels
+
+
+def vmem(limit):
+    return pltpu.CompilerParams(vmem_limit_bytes=limit)
+
+
+def exchange(matrix, pivots):
+    height, width = matrix.shape
+    row_groups, col_groups = lax.axis_size("prow"), lax.axis_size("pcol")
+    row_me, col_me = lax.axis_index("prow"), lax.axis_index("pcol")
+    outer, inner = grid_of(row_groups)
+    cap = round_rows(row_groups)
+    shape = jax.ShapeDtypeStruct
+    smem = pl.BlockSpec(memory_space=pltpu.SMEM)
+
+    panel = spread(matrix[:, :NB], "pcol", col_me, tree(col_groups))
+    both = ("prow", "pcol")
+    me = row_me * col_groups + col_me
+    block = spread(matrix[:NB, :NB], both, me, tree(row_groups, col_groups))
+    block = spread(block, "pcol", col_me, tree(col_groups))
+
+    source, landing = pl.pallas_call(
+        plan_kernel,
+        out_shape=[shape((1, NB), I32)] * 2,
+        in_specs=[smem],
+        out_specs=[smem, smem],
+        scratch_shapes=[pltpu.SMEM((height * row_groups,), I32)],
+        name="plan",
+    )(pivots)
+
+    whole = pl.BlockSpec(memory_space=pltpu.VMEM)
+    rows, gather, place, flag, *gives = pl.pallas_call(
+        functools.partial(pick_kernel, row_groups, cap),
+        out_shape=[
+            shape((cap, width), BF16),
+            shape((NB, row_groups * cap), BF16),
+            shape((1, HALF), I32),
+            shape((1, HALF), I32),
+        ]
+        + [shape((outer * cap, width), BF16)] * inner,
+        in_specs=[whole] * 3,
+        out_specs=[whole] * (4 + inner),
+        compiler_params=vmem(40 << 20),
+        name="pick",
+    )(source, landing, matrix)
+
+    def at(o, i):
+        return o % outer * inner + i % inner
+
+    everyone = [(o, i) for o in range(outer) for i in range(inner)]
+    parts = [rows]
+    for step in range(1, outer):
+        parts.append(lax.ppermute(rows, "prow", [(at(o, i), at(o + step, i)) for o, i in everyone]))
+    for turn in range(1, inner):
+        pairs = [(at(o, i), at(o, i + turn)) for o, i in everyone]
+        parts += [lax.ppermute(part, "prow", pairs) for part in parts[:outer]]
+
+    held = gives[0]
+    for j in range(1, inner):
+        held = jnp.where(row_me == j, lax.ppermute(gives[j], "prow", [(0, j)]), held)
+    arrived = [held[:cap]]
+    for step in range(1, outer):
+        piece = held[step * cap : (step + 1) * cap]
+        arrived.append(lax.ppermute(piece, "prow", [(i, at(step, i)) for i in range(inner)]))
+
+    inverse = pl.pallas_call(
+        invert_kernel,
+        out_shape=shape((NB, HALF), F32),
+        in_specs=[whole],
+        out_specs=whole,
+        name="invert",
+    )(block)
+
+    def full(x):
+        return pl.BlockSpec(x.shape, lambda j: (0, 0))
+
+    def columns(x):
+        return pl.BlockSpec((x.shape[0], NB), lambda j: (0, j))
+
+    result = pl.pallas_call(
+        functools.partial(finish_kernel, row_groups, cap),
+        out_shape=shape(matrix.shape, BF16),
+        grid=(width // NB,),
+        in_specs=[columns(matrix)]
+        + [full(x) for x in (block, inverse, panel, gather, place)]
+        + [columns(x) for x in (*parts, *arrived)],
+        out_specs=columns(matrix),
+        scratch_shapes=[
+            pltpu.VMEM((height, NB + cap), BF16),
+            pltpu.VMEM((height, HALF), F32),
+            pltpu.VMEM((HALF, 3 * HALF), BF16),
+            pltpu.VMEM((HALF, 3 * HALF), BF16),
+            pltpu.VMEM((HALF, 6 * HALF), BF16),
+        ],
+        compiler_params=vmem(40 << 20),
+        name="finish",
+    )(matrix, block, inverse, panel, gather, place, *parts, *arrived)
+    return result, flag[0, 0] > cap
 
 
 def broadcast(block, axis, owner):
@@ -37,7 +338,7 @@
     return (top_anchor, wanted_anchor)
 
 
-def local(matrix, pivots):
+def general(matrix, pivots):
     rows_local, cols_local = matrix.shape
     row_groups = lax.axis_size("prow")
     prow_index = lax.axis_index("prow")
@@ -70,6 +371,15 @@
     return jnp.where(panel_column[None, :], matrix, result)
 
 
+def local(matrix, pivots):
+    result, too_many = exchange(matrix, pivots)
+
+    def again(state):
+        return jnp.zeros((), jnp.bool_), general(matrix, pivots)
+
+    return lax.while_loop(lambda state: state[0], again, (too_many, result))[1]
+
+
 def solution(mesh):
     placed = (P("prow", "pcol"), P())
     return jax.shard_map(

time: 213 us -> 108 us (0.51)
  the two profiles are of different devices: /device:TPU:6 before, /device:TPU:26 now
where the time goes in v1:
time: 108 us; the launch traced here: 107 us
  waiting for transfers between devices  32.2 us (30%)
  Pallas kernels  30.8 us (29%)
  starting transfers between devices  17.5 us (16%)
  between operations  13.7 us (13%)
  other arithmetic  9.26 us (9%)
  local copies, waits for them, and re-layouts  3.57 us (3%)
    ppermute x7, waiting for transfers between devices, spread(): received = lax.ppermute(value, axes, pairs)  20.9 us
    pallas_call x1, Pallas kernels, exchange(): pl.pallas_call(functools.partial(finish_kernel, row_groups, cap), out_sha...  14 us
    ppermute x3, waiting for transfers between devices, exchange(): lax.ppermute(piece, 'prow', [(i, at(step, i)) for i in range(inner)])  11.3 us
    pallas_call x1, Pallas kernels, exchange(): pl.pallas_call(invert_kernel, out_shape=shape((NB, HALF), F32), in_specs=...  8.02 us
    ppermute x7, starting transfers between devices, spread(): received = lax.ppermute(value, axes, pairs)  7.24 us
    select_n x7, other arithmetic, spread(): value = jnp.where(jnp.any(index == takers), received, value)  5.85 us
    pallas_call x1, Pallas kernels, exchange(): pl.pallas_call(functools.partial(pick_kernel, row_groups, cap), out_shape...  4.78 us
    pallas_call x1, Pallas kernels, exchange(): pl.pallas_call(plan_kernel, out_shape=[shape((1, NB), I32)] * 2, in_specs...  4.08 us
  transfers between devices with their start and end apart: 18, of which 3 were waited for; matrix products, arithmetic and copies ran while one was open for 8% of the time, Pallas kernels for 16%

profile of v1, /device:TPU:26, one launch (start us, length us, event | category | flops | bytes accessed | tf_op | source)
XLA Modules:
  0.0 107.1 jit_solution(17210759281862298880)
XLA Ops:
  6.5 0.9 slice.45
  7.5 0.7 collective-permute-start
  8.2 0.0 collective-permute-done
  8.2 0.9 broadcast_select_fusion.4
  9.1 0.7 collective-permute-start.1
  9.8 1.3 %compare_reduce_fusion = pred[]{:T(512)} fusion(s32[2]{0:T(128)} %constant.158.clone, s32[]{:T(128)S(6)} %add.371), kind=kLoop, calls=%fused_computation.158 | loop fusion | flops 3 | bytes 13 | tf_op jit(solution)/shard_map/reduce_or | solution.py:200
  11.1 0.0 collective-permute-done.1
  11.1 0.7 broadcast_select_fusion.6
  11.7 0.7 collective-permute-start.2
  12.4 1.2 %slice.46 = bf16[1792,256]{1,0:T(8,128)(2,1)S(1)} slice(bf16[1792,1792]{1,0:T(8,128)(2,1)} %refs_0_.1), slice={[0:1792], [0:256]} | slice | bytes 1835008 | tf_op jit(solution)/shard_map/slice | solution.py:225
  13.7 1.3 %collective-permute-start.5 = (bf16[1792,256]{1,0:T(8,128)(2,1)S(1)}, bf16[1792,256]{1,0:T(8,128)(2,1)}, u32[]{:S(2)}, u32[]{:S(2)}) collective-permute-start(bf16[1792,256]{1,0:T(8,128)(2,1)S(1)} %slice.46), channel_id=1, source_target_pairs={{0,2},{4,6},{8,10},{12,14},{16,18},{20,22},{24,26},{28,30}} | collective-permute-start | bytes 2752520 | tf_op jit(solution)/shard_map/ppermute | solution.py:198
  15.0 1.3 %compare_reduce_fusion.1 = pred[]{:T(512)} fusion(s32[4]{0:T(128)} %constant.159.clone, s32[]{:T(128)S(6)} %add.371), kind=kLoop, calls=%fused_computation.159 | loop fusion | flops 7 | bytes 21 | tf_op jit(solution)/shard_map/reduce_or | solution.py:200
  16.3 0.0 collective-permute-done.2
  16.3 0.7 broadcast_select_fusion.7
  16.9 1.3 %collective-permute-start.3 = (bf16[256,256]{1,0:T(8,128)(2,1)S(1)}, bf16[256,256]{1,0:T(8,128)(2,1)S(1)}, u32[]{:S(2)}, u32[]{:S(2)}) collective-permute-start(bf16[256,256]{1,0:T(8,128)(2,1)S(1)} %broadcast_select_fusion.7), channel_id=1, source_target_pairs={{0,2},{4,6},{8,10},{12,14},{16,18},{20,22},{24,26},{28,30}} | collective-permute-start | bytes 393224 | tf_op jit(solution)/shard_map/ppermute | solution.py:198
  18.2 20.4 %collective-permute-done.3 = bf16[256,256]{1,0:T(8,128)(2,1)S(1)} collective-permute-done((bf16[256,256]{1,0:T(8,128)(2,1)S(1)}, bf16[256,256]{1,0:T(8,128)(2,1)S(1)}, u32[]{:S(2)}, u32[]{:S(2)}) %collective-permute-start.3) | collective-permute-done | bytes 131104 | tf_op jit(solution)/shard_map/ppermute | solution.py:198
  38.6 1.3 %collective-permute-start.4 = (bf16[256,256]{1,0:T(8,128)(2,1)S(1)}, bf16[256,256]{1,0:T(8,128)(2,1)S(1)}, u32[]{:S(2)}, u32[]{:S(2)}) collective-permute-start(bf16[256,256]{1,0:T(8,128)(2,1)S(1)} %broadcast_select_fusion.5), channel_id=1, source_target_pairs={{0,1},{2,3},{4,5},{6,7},{8,9},{10,11},{12,13},{14,15},{16,17},{18,... | collective-permute-start | bytes 393224 | tf_op jit(solution)/shard_map/ppermute | solution.py:198
  40.0 4.1 %plan.1 = (s32[1,256]{1,0:T(1,128)}, s32[1,256]{1,0:T(1,128)}) custom-call(s32[256]{0:T(256)} %pivots.1), custom_call_target="tpu_custom_call" | custom-call | tf_op jit(solution)/shard_map/plan/pallas_call | solution.py:231
  44.0 0.0 copy-start.2
  44.1 0.7 copy-done.2
  44.7 0.7 copy-done.3
  45.4 4.8 %pick.1 = (bf16[48,1792]{1,0:T(8,128)(2,1)S(1)}, bf16[256,384]{1,0:T(8,128)(2,1)S(1)}, s32[1,128]{1,0:T(1,128)S(1)}, s32[1,128]{1,0:T(1,128)S(1)}, bf16[192,1792...) custom-call(s32[1,256]{1,0:T(1,128)S(1)} %copy-done.2, s32[1,256]{1,0:T(1,128)S(1)} %copy-done.3, bf16[1792,1792]{1,0:T(8,128)(2,1)} %refs_0_.1), custom_call_target="tpu_custom_call" | custom-call | tf_op jit(solution)/shard_map/pick/pallas_call | solution.py:241
  50.2 0.1 collective-permute-start.7
  50.2 1.0 collective-permute-start.8
  51.3 1.0 collective-permute-start.9
  52.3 0.7 compare_reduce_fusion.2
  53.0 1.6 %collective-permute-start.14 = (bf16[192,1792]{1,0:T(8,128)(2,1)S(1)}, bf16[192,1792]{1,0:T(8,128)(2,1)}, u32[]{:S(2)}, u32[]{:S(2)}) collective-permute-start(bf16[192,1792]{1,0:T(8,128)(2,1)S(1)} %get-tuple-element.39), channel_id=1, source_target_pairs={{0,4},{1,5},{2,6},{3,7}} | collective-permute-start | bytes 2064392 | tf_op jit(solution)/shard_map/ppermute | solution.py:269
  54.6 1.3 %broadcast_select_fusion.8.block.refs_1_ = bf16[256,256]{1,0:T(8,128)(2,1)} fusion(bf16[256,256]{1,0:T(8,128)(2,1)S(1)} %collective-permute-done.4, bf16[256,256]{1,0:T(8,128)(2,1)S(1)} %broadcast_select_fusion.5, pred[]{:T(512)} %compare_reduce_fusion.2), kind=kLoop, calls=%fused_computation.157 | loop fusion | flops 65536 | bytes 393217 | tf_op jit(solution)/shard_map/jit(_where)/select_n | solution.py:200
  55.9 8.0 %invert.1.refs_2_ = f32[256,128]{1,0:T(8,128)} custom-call(bf16[256,256]{1,0:T(8,128)(2,1)} %broadcast_select_fusion.8.block.refs_1_), custom_call_target="tpu_custom_call" | custom-call | tf_op jit(solution)/shard_map/invert/pallas_call | solution.py:275
  63.9 0.0 collective-permute-done.8.refs_8_
  63.9 2.0 %collective-permute-start.11 = (bf16[48,1792]{1,0:T(8,128)(2,1)S(1)}, bf16[48,1792]{1,0:T(8,128)(2,1)S(1)}, u32[]{:S(2)}, u32[]{:S(2)}) collective-permute-start(bf16[48,1792]{1,0:T(8,128)(2,1)S(1)} %collective-permute-done.7.refs_7_), channel_id=1, source_target_pairs={{0,4},{4,0},{8,12},{12,8},{16,20},{20,16},{24,28},{28,24},{1,5},{5... | collective-permute-start | bytes 516104 | tf_op jit(solution)/shard_map/ppermute | solution.py:265
  65.9 0.0 collective-permute-done.9.refs_9_
  65.9 0.1 collective-permute-start.12
  66.0 0.0 collective-permute-done.5
  66.0 1.9 %collective-permute-start.13 = (bf16[48,1792]{1,0:T(8,128)(2,1)S(1)}, bf16[48,1792]{1,0:T(8,128)(2,1)S(1)}, u32[]{:S(2)}, u32[]{:S(2)}) collective-permute-start(bf16[48,1792]{1,0:T(8,128)(2,1)S(1)} %collective-permute-done.9.refs_9_), channel_id=1, source_target_pairs={{0,4},{4,0},{8,12},{12,8},{16,20},{20,16},{24,28},{28,24},{1,5},{5... | collective-permute-start | bytes 516104 | tf_op jit(solution)/shard_map/ppermute | solution.py:265
  68.0 1.6 %broadcast_select_fusion.1 = bf16[1792,256]{1,0:T(8,128)(2,1)S(1)} fusion(bf16[1792,256]{1,0:T(8,128)(2,1)} %collective-permute-done.5, pred[]{:T(512)S(6)} %eq.116, bf16[1792,1792]{1,0:T(8,128)(2,1)} %refs_0_.1), kind=kLoop, calls=%fused_computation.150 | loop fusion | flops 458752 | bytes 2752513 | tf_op jit(solution)/shard_map/jit(_where)/select_n | solution.py:200
  69.5 0.0 collective-permute-done.14
  69.5 1.3 %collective-permute-start.6 = (bf16[1792,256]{1,0:T(8,128)(2,1)S(1)}, bf16[1792,256]{1,0:T(8,128)(2,1)S(1)}, u32[]{:S(2)}, u32[]{:S(2)}) collective-permute-start(bf16[1792,256]{1,0:T(8,128)(2,1)S(1)} %broadcast_select_fusion.1), channel_id=1, source_target_pairs={{0,1},{2,3},{4,5},{6,7},{8,9},{10,11},{12,13},{14,15},{16,17},{18,... | collective-permute-start | bytes 2752520 | tf_op jit(solution)/shard_map/ppermute | solution.py:198
  70.9 0.1 broadcast_select_fusion.3
  71.1 0.0 collective-permute-done.10.refs_10_
  71.1 0.7 collective-permute-start.15
  71.8 0.0 collective-permute-done.11.refs_11_
  71.8 0.7 collective-permute-start.16
  72.4 0.5 collective-permute-done.6
  72.9 1.3 %collective-permute-start.17 = (bf16[48,1792]{1,0:T(8,128)(2,1)S(1)}, bf16[48,1792]{1,0:T(8,128)(2,1)S(1)}, u32[]{:S(2)}, u32[]{:S(2)}) collective-permute-start(bf16[48,1792]{1,0:T(8,128)(2,1)S(1)} %get-tuple-element.82), channel_id=1, source_target_pairs={{0,24},{4,28},{1,25},{5,29},{2,26},{6,30},{3,27},{7,31}} | collective-permute-start | bytes 516104 | tf_op jit(solution)/shard_map/ppermute | solution.py:273
  74.2 0.7 broadcast_select_fusion.2.refs_3_
  75.0 11.3 %collective-permute-done.17.refs_17_ = bf16[48,1792]{1,0:T(8,128)(2,1)S(1)} collective-permute-done((bf16[48,1792]{1,0:T(8,128)(2,1)S(1)}, bf16[48,1792]{1,0:T(8,128)(2,1)S(1)}, u32[]{:S(2)}, u32[]{:S(2)}) %collective-permute-start.17) | collective-permute-done | bytes 172064 | tf_op jit(solution)/shard_map/ppermute | solution.py:273
  86.3 14.0 %finish.1 = bf16[1792,1792]{1,0:T(8,128)(2,1)} custom-call(bf16[1792,1792]{1,0:T(8,128)(2,1)} %refs_0_.1, bf16[256,256]{1,0:T(8,128)(2,1)S(1)} %copy-done, f32[256,128]{1,0:T(8,128)S(1)} %copy-done.1, bf16[1792,256]{1,0:T(8,128)(2,1)S(1)} %broadcast_select_fusion.2.refs_3_, bf16[256,384]{1,0:T(8,128)(2,1)S(1)} %get-tuple-element.36.refs_4_, ...), custom_call_target="tpu_custom_call" | custom-call | tf_op jit(solution)/shard_map/finish/pallas_call | solution.py:289
  (19 shorter events, 0.1 us)
Async XLA Ops:
  6.5 45.8 %copy-start.7 = (s32[2]{0:T(128)S(1)}, s32[2]{0:T(128)}, u32[]{:S(2)}) copy-start(s32[2]{0:T(128)} %constant.156.clone) | copy-start | bytes 28
  7.5 0.7 collective-permute-start
  9.1 2.0 %collective-permute-start.1 = (bf16[256,256]{1,0:T(8,128)(2,1)S(1)}, bf16[256,256]{1,0:T(8,128)(2,1)S(1)}, u32[]{:S(2)}, u32[]{:S(2)}) collective-permute-start(bf16[256,256]{1,0:T(8,128)(2,1)S(1)} %broadcast_select_fusion.4), channel_id=1, source_target_pairs={{0,8},{16,24}} | collective-permute-start | bytes 393224 | tf_op jit(solution)/shard_map/ppermute | solution.py:198
  11.7 4.5 %collective-permute-start.2 = (bf16[256,256]{1,0:T(8,128)(2,1)S(1)}, bf16[256,256]{1,0:T(8,128)(2,1)S(1)}, u32[]{:S(2)}, u32[]{:S(2)}) collective-permute-start(bf16[256,256]{1,0:T(8,128)(2,1)S(1)} %broadcast_select_fusion.6), channel_id=1, source_target_pairs={{0,4},{8,12},{16,20},{24,28}} | collective-permute-start | bytes 393224 | tf_op jit(solution)/shard_map/ppermute | solution.py:198
  13.7 52.4 %collective-permute-start.5 = (bf16[1792,256]{1,0:T(8,128)(2,1)S(1)}, bf16[1792,256]{1,0:T(8,128)(2,1)}, u32[]{:S(2)}, u32[]{:S(2)}) collective-permute-start(bf16[1792,256]{1,0:T(8,128)(2,1)S(1)} %slice.46), channel_id=1, source_target_pairs={{0,2},{4,6},{8,10},{12,14},{16,18},{20,22},{24,26},{28,30}} | collective-permute-start | bytes 2752520 | tf_op jit(solution)/shard_map/ppermute | solution.py:198
  16.9 21.7 %collective-permute-start.3 = (bf16[256,256]{1,0:T(8,128)(2,1)S(1)}, bf16[256,256]{1,0:T(8,128)(2,1)S(1)}, u32[]{:S(2)}, u32[]{:S(2)}) collective-permute-start(bf16[256,256]{1,0:T(8,128)(2,1)S(1)} %broadcast_select_fusion.7), channel_id=1, source_target_pairs={{0,2},{4,6},{8,10},{12,14},{16,18},{20,22},{24,26},{28,30}} | collective-permute-start | bytes 393224 | tf_op jit(solution)/shard_map/ppermute | solution.py:198
  38.6 14.4 %collective-permute-start.4 = (bf16[256,256]{1,0:T(8,128)(2,1)S(1)}, bf16[256,256]{1,0:T(8,128)(2,1)S(1)}, u32[]{:S(2)}, u32[]{:S(2)}) collective-permute-start(bf16[256,256]{1,0:T(8,128)(2,1)S(1)} %broadcast_select_fusion.5), channel_id=1, source_target_pairs={{0,1},{2,3},{4,5},{6,7},{8,9},{10,11},{12,13},{14,15},{16,17},{18,... | collective-permute-start | bytes 393224 | tf_op jit(solution)/shard_map/ppermute | solution.py:198
  44.0 0.7 copy-start.2
  44.7 0.7 copy-start.3
  50.2 13.7 %collective-permute-start.7 = (bf16[48,1792]{1,0:T(8,128)(2,1)S(1)}, bf16[48,1792]{1,0:T(8,128)(2,1)S(1)}, u32[]{:S(2)}, u32[]{:S(2)}) collective-permute-start(bf16[48,1792]{1,0:T(8,128)(2,1)S(1)} %get-tuple-element.38.refs_6_), channel_id=1, source_target_pairs={{0,8},{4,12},{8,16},{12,20},{16,24},{20,28},{24,0},{28,4},{1,9},{5... | collective-permute-start | bytes 516104 | tf_op jit(solution)/shard_map/ppermute | solution.py:262
  50.2 13.7 %collective-permute-start.8 = (bf16[48,1792]{1,0:T(8,128)(2,1)S(1)}, bf16[48,1792]{1,0:T(8,128)(2,1)S(1)}, u32[]{:S(2)}, u32[]{:S(2)}) collective-permute-start(bf16[48,1792]{1,0:T(8,128)(2,1)S(1)} %get-tuple-element.38.refs_6_), channel_id=1, source_target_pairs={{0,16},{4,20},{8,24},{12,28},{16,0},{20,4},{24,8},{28,12},{1,17},{... | collective-permute-start | bytes 516104 | tf_op jit(solution)/shard_map/ppermute | solution.py:262
  51.3 14.7 %collective-permute-start.9 = (bf16[48,1792]{1,0:T(8,128)(2,1)S(1)}, bf16[48,1792]{1,0:T(8,128)(2,1)S(1)}, u32[]{:S(2)}, u32[]{:S(2)}) collective-permute-start(bf16[48,1792]{1,0:T(8,128)(2,1)S(1)} %get-tuple-element.38.refs_6_), channel_id=1, source_target_pairs={{0,24},{4,28},{8,0},{12,4},{16,8},{20,12},{24,16},{28,20},{1,25},{... | collective-permute-start | bytes 516104 | tf_op jit(solution)/shard_map/ppermute | solution.py:262
  53.0 16.5 %collective-permute-start.14 = (bf16[192,1792]{1,0:T(8,128)(2,1)S(1)}, bf16[192,1792]{1,0:T(8,128)(2,1)}, u32[]{:S(2)}, u32[]{:S(2)}) collective-permute-start(bf16[192,1792]{1,0:T(8,128)(2,1)S(1)} %get-tuple-element.39), channel_id=1, source_target_pairs={{0,4},{1,5},{2,6},{3,7}} | collective-permute-start | bytes 2064392 | tf_op jit(solution)/shard_map/ppermute | solution.py:269
  55.9 30.4 %copy-start = (bf16[256,256]{1,0:T(8,128)(2,1)S(1)}, bf16[256,256]{1,0:T(8,128)(2,1)}, u32[]{:S(2)}) copy-start(bf16[256,256]{1,0:T(8,128)(2,1)} %broadcast_select_fusion.8.block.refs_1_) | copy-start | bytes 393220
  63.9 22.4 %copy-start.1 = (f32[256,128]{1,0:T(8,128)S(1)}, f32[256,128]{1,0:T(8,128)}, u32[]{:S(2)}) copy-start(f32[256,128]{1,0:T(8,128)} %invert.1.refs_2_) | copy-start | bytes 393220
  63.9 7.2 %collective-permute-start.10 = (bf16[48,1792]{1,0:T(8,128)(2,1)S(1)}, bf16[48,1792]{1,0:T(8,128)(2,1)S(1)}, u32[]{:S(2)}, u32[]{:S(2)}) collective-permute-start(bf16[48,1792]{1,0:T(8,128)(2,1)S(1)} %get-tuple-element.38.refs_6_), channel_id=1, source_target_pairs={{0,4},{4,0},{8,12},{12,8},{16,20},{20,16},{24,28},{28,24},{1,5},{5... | collective-permute-start | bytes 516104 | tf_op jit(solution)/shard_map/ppermute | solution.py:265
  63.9 7.8 %collective-permute-start.11 = (bf16[48,1792]{1,0:T(8,128)(2,1)S(1)}, bf16[48,1792]{1,0:T(8,128)(2,1)S(1)}, u32[]{:S(2)}, u32[]{:S(2)}) collective-permute-start(bf16[48,1792]{1,0:T(8,128)(2,1)S(1)} %collective-permute-done.7.refs_7_), channel_id=1, source_target_pairs={{0,4},{4,0},{8,12},{12,8},{16,20},{20,16},{24,28},{28,24},{1,5},{5... | collective-permute-start | bytes 516104 | tf_op jit(solution)/shard_map/ppermute | solution.py:265
  65.9 9.0 %collective-permute-start.12 = (bf16[48,1792]{1,0:T(8,128)(2,1)S(1)}, bf16[48,1792]{1,0:T(8,128)(2,1)S(1)}, u32[]{:S(2)}, u32[]{:S(2)}) collective-permute-start(bf16[48,1792]{1,0:T(8,128)(2,1)S(1)} %collective-permute-done.8.refs_8_), channel_id=1, source_target_pairs={{0,4},{4,0},{8,12},{12,8},{16,20},{20,16},{24,28},{28,24},{1,5},{5... | collective-permute-start | bytes 516104 | tf_op jit(solution)/shard_map/ppermute | solution.py:265
  66.0 8.9 %collective-permute-start.13 = (bf16[48,1792]{1,0:T(8,128)(2,1)S(1)}, bf16[48,1792]{1,0:T(8,128)(2,1)S(1)}, u32[]{:S(2)}, u32[]{:S(2)}) collective-permute-start(bf16[48,1792]{1,0:T(8,128)(2,1)S(1)} %collective-permute-done.9.refs_9_), channel_id=1, source_target_pairs={{0,4},{4,0},{8,12},{12,8},{16,20},{20,16},{24,28},{28,24},{1,5},{5... | collective-permute-start | bytes 516104 | tf_op jit(solution)/shard_map/ppermute | solution.py:265
  69.5 3.4 %collective-permute-start.6 = (bf16[1792,256]{1,0:T(8,128)(2,1)S(1)}, bf16[1792,256]{1,0:T(8,128)(2,1)S(1)}, u32[]{:S(2)}, u32[]{:S(2)}) collective-permute-start(bf16[1792,256]{1,0:T(8,128)(2,1)S(1)} %broadcast_select_fusion.1), channel_id=1, source_target_pairs={{0,1},{2,3},{4,5},{6,7},{8,9},{10,11},{12,13},{14,15},{16,17},{18,... | collective-permute-start | bytes 2752520 | tf_op jit(solution)/shard_map/ppermute | solution.py:198
  71.1 3.9 %collective-permute-start.15 = (bf16[48,1792]{1,0:T(8,128)(2,1)S(1)}, bf16[48,1792]{1,0:T(8,128)(2,1)S(1)}, u32[]{:S(2)}, u32[]{:S(2)}) collective-permute-start(bf16[48,1792]{1,0:T(8,128)(2,1)S(1)} %get-tuple-element.84), channel_id=1, source_target_pairs={{0,8},{4,12},{1,9},{5,13},{2,10},{6,14},{3,11},{7,15}} | collective-permute-start | bytes 516104 | tf_op jit(solution)/shard_map/ppermute | solution.py:273
  71.8 3.2 %collective-permute-start.16 = (bf16[48,1792]{1,0:T(8,128)(2,1)S(1)}, bf16[48,1792]{1,0:T(8,128)(2,1)S(1)}, u32[]{:S(2)}, u32[]{:S(2)}) collective-permute-start(bf16[48,1792]{1,0:T(8,128)(2,1)S(1)} %get-tuple-element.83), channel_id=1, source_target_pairs={{0,16},{4,20},{1,17},{5,21},{2,18},{6,22},{3,19},{7,23}} | collective-permute-start | bytes 516104 | tf_op jit(solution)/shard_map/ppermute | solution.py:273
  72.9 13.3 %collective-permute-start.17 = (bf16[48,1792]{1,0:T(8,128)(2,1)S(1)}, bf16[48,1792]{1,0:T(8,128)(2,1)S(1)}, u32[]{:S(2)}, u32[]{:S(2)}) collective-permute-start(bf16[48,1792]{1,0:T(8,128)(2,1)S(1)} %get-tuple-element.82), channel_id=1, source_target_pairs={{0,24},{4,28},{1,25},{5,29},{2,26},{6,30},{3,27},{7,31}} | collective-permute-start | bytes 516104 | tf_op jit(solution)/shard_map/ppermute | solution.py:273
  86.3 14.0 %copy-start.6 = (s32[256]{0:T(256)S(1)}, s32[256]{0:T(256)}, u32[]{:S(2)}) copy-start(s32[256]{0:T(256)} %pivots.1) | copy-start | bytes 3076

commit v2 on v0

v2 whole, which is shorter than its diff:
```python
import functools

import jax
import jax.numpy as jnp
from jax import lax
from jax.experimental import pallas as pl
from jax.experimental.pallas import tpu as pltpu
from jax.sharding import PartitionSpec as P

NB = 256
HALF = 128
BF16 = jnp.bfloat16
F32 = jnp.float32
I32 = jnp.int32


def grid_of(row_groups):
    outer = 4 if row_groups % 4 == 0 else row_groups
    return outer, row_groups // outer


def round_rows(row_groups):
    share = -(-3 * NB // (2 * row_groups))
    return min(NB, -(-share // 16) * 16)


def iota(shape, dim):
    return lax.broadcasted_iota(I32, shape, dim)


def dot(a, b):
    return jnp.dot(a, b, preferred_element_type=F32)


def block_owner(global_row, row_groups):
    block = lax.shift_right_logical(global_row, 8)
    if row_groups & (row_groups - 1) == 0:
        return block & (row_groups - 1), lax.shift_right_logical(block, row_groups.bit_length() - 1)
    return lax.rem(block, row_groups), lax.div(block, row_groups)


def place_of(source, row_groups):
    owner, block = block_owner(source, row_groups)
    return owner, block * NB + (source & (NB - 1))


def follow_swaps(pivots, anchor, source, landing):
    def start(k, _):
        anchor[pivots[k]] = pivots[k]
        return 0

    def swap(k, _):
        target = pivots[k]
        at_column, at_target = anchor[k], anchor[target]
        anchor[k] = at_target
        anchor[target] = at_column
        return 0

    def write(k, _):
        row = anchor[k]
        source[0, k] = row
        landing[0, k] = jnp.where(row >= NB, anchor[row], -1)
        return 0

    lax.fori_loop(0, NB, start, 0, unroll=16)
    for k in range(NB):
        anchor[k] = k
    lax.fori_loop(0, NB, swap, 0, unroll=16)
    lax.fori_loop(0, NB, write, 0, unroll=16)


def as_column(row):
    n = row.shape[1]
    wide = jnp.broadcast_to(row, (n, n))
    on_diagonal = iota((n, n), 0) == iota((n, n), 1)
    return jnp.sum(jnp.where(on_diagonal, wide, 0), axis=1, keepdims=True)


def pick_kernel(row_groups, cap, pivots, matrix, rows, source_out, landing_out, *scratch):
    held, anchor, source, landing, source_sem, landing_sem, sems = scratch
    height = matrix.shape[0]
    loads = []
    for i in range(height // NB):
        part = pl.ds(i * NB, NB)
        loads.append(pltpu.make_async_copy(matrix.at[part], held.at[part], sems.at[i]))
        loads[-1].start()
    follow_swaps(pivots, anchor, source, landing)
    one = pltpu.make_async_copy(source, source_out, source_sem)
    two = pltpu.make_async_copy(landing, landing_out, landing_sem)
    one.start()
    two.start()
    one.wait()
    two.wait()
    me = lax.axis_index("prow")
    owner, local = place_of(source_out[...], row_groups)
    slot, _ = slots_of(owner, row_groups)
    hit = (slot == iota((cap, NB), 0)) & (owner == me)
    my_rows = jnp.max(jnp.where(hit, local, -1), axis=1, keepdims=True)
    for load in loads:
        load.wait()
    chosen = (my_rows == iota((cap, height), 1)).astype(BF16)
    rows[...] = dot(chosen, held[...]).astype(BF16)


def slots_of(owner, row_groups):
    is_owner = (iota((row_groups, NB), 0) == owner).astype(BF16)
    upto = (iota((NB, NB), 0) <= iota((NB, NB), 1)).astype(BF16)
    ranks = dot(is_owner, upto)
    slot = jnp.sum(jnp.where(is_owner > 0, ranks, 0.0), axis=0, keepdims=True).astype(I32) - 1
    return slot, jnp.max(ranks, axis=(0, 1), keepdims=True).astype(I32)


def tables_kernel(row_groups, cap, source, landing, old_top, gather, place, flag, *gives):
    outer, inner = grid_of(row_groups)
    me = lax.axis_index("prow")
    land = landing[...]
    owner, local = place_of(source[...], row_groups)
    slot, most = slots_of(owner, row_groups)
    flag[...] = jnp.broadcast_to(most, flag.shape)
    code = jnp.where(slot < cap, owner * cap + slot, -1)
    for j in range(inner):
        wanted = []
        for z in range(outer):
            hit = code == iota((cap, NB), 0) + (z * inner + j) * cap
            wanted.append(jnp.max(jnp.where(hit, land, -1), axis=1, keepdims=True))
        chosen_top = (jnp.concatenate(wanted, 0) == iota((outer * cap, NB), 1)).astype(BF16)
        gives[j][...] = dot(chosen_top, old_top[...]).astype(BF16)
    code_column = as_column(code)
    lands_column = as_column(jnp.where(land >= 0, local, -1))
    mine = code_column - me * cap == iota((NB, HALF), 1)
    mine = mine & (iota((NB, HALF), 1) < cap)
    place[...] = jnp.max(jnp.where(mine, lands_column, -1), axis=0, keepdims=True)
    my_outer, my_inner = me // inner, me % inner
    for turn in range(inner):
        for step in range(outer):
            from_outer = lax.rem(my_outer - step + outer, outer)
            from_inner = lax.rem(my_inner - turn + inner, inner)
            first = (from_outer * inner + from_inner) * cap
            at = (turn * outer + step) * cap
            gather[:, at : at + cap] = (code_column == iota((NB, cap), 1) + first).astype(BF16)


def pick_all_kernel(row_groups, source, landing, matrix, rows, place):
    owner, local = place_of(source[...], row_groups)
    mine = owner == lax.axis_index("prow")
    wanted = as_column(jnp.where(mine, local, -1))
    chosen = (wanted == iota((NB, matrix.shape[0]), 1)).astype(BF16)
    rows[...] = dot(chosen, matrix[...]).astype(BF16)
    from_top = as_column(jnp.where(mine, landing[...], -1)) == iota((NB, NB), 1)
    place[...] = jnp.max(jnp.where(from_top, wanted, -1), axis=0, keepdims=True)


def pieces(x):
    high = x.astype(BF16)
    rest = x - high.astype(F32)
    middle = rest.astype(BF16)
    return high, middle, (rest - middle.astype(F32)).astype(BF16)


def invert_kernel(block, inverse):
    rows, cols = iota((NB, NB), 0), iota((NB, NB), 1)
    apart = rows ^ cols
    lower = jnp.where(rows > cols, block[...], jnp.zeros((), BF16))

    def corner(size):
        return jnp.where((apart >= size) & (apart < 2 * size), lower, jnp.zeros((), BF16))

    x = jnp.where(rows == cols, 1.0, 0.0) - corner(1).astype(F32)
    size = 2
    while size < HALF:
        high, middle, low = pieces(x)
        edge = corner(size)
        inner = (dot(edge, low) + dot(edge, middle)) + dot(edge, high)
        first, second, third = pieces(inner)
        small = (dot(high, third) + dot(low, first)) + dot(middle, second)
        x = x - ((small + (dot(high, second) + dot(middle, first))) + dot(high, first))
        size *= 2
    inverse[:HALF] = x[:HALF, :HALF]
    inverse[HALF:] = x[HALF:, HALF:]


def prepare_kernel(swaps, mine, received, place, left, keep):
    row_me, col_me = lax.axis_index("prow"), lax.axis_index("pcol")
    height = left.shape[0]

    @pl.when(col_me % 2 == 0)
    def _():
        left[:, :NB] = -mine[:height]

    @pl.when(col_me % 2 == 1)
    def _():
        left[:, :NB] = -received[:height]

    hit = iota((height, place.shape[1]), 0) == place[...]
    left[:, NB:] = hit[:, :swaps].astype(BF16)
    kept = jnp.max(jnp.where(hit, 1.0, 0.0), axis=1, keepdims=True) == 0.0
    keep[...] = jnp.where(jnp.broadcast_to(kept, keep.shape), 1.0, 0.0).astype(BF16)

    @pl.when(row_me == 0)
    def _():
        keep[:NB] = jnp.zeros((NB, HALF), BF16)
        left[:NB, :NB] = (iota((NB, NB), 0) == iota((NB, NB), 1)).astype(BF16)
        left[:NB, NB:] = jnp.zeros((NB, swaps), BF16)


def solve_kernel(block, inverse, gather, *refs):
    parts, upper = refs[:-1], refs[-1]
    rows = jnp.concatenate([part[...] for part in parts], 0)
    top = dot(gather[...], rows)
    top1 = top[:HALF].astype(BF16)
    first = jnp.concatenate(pieces(inverse[:HALF]), 1)
    upper1 = dot(first, jnp.concatenate([top1] * 3, 0))
    edge = block[HALF:, :HALF]
    edges = jnp.concatenate([edge, edge, edge], 1)
    rest = top[HALF:] - dot(edges, jnp.concatenate(pieces(upper1), 0))
    x, y, z = pieces(inverse[HALF:])
    high, middle, low = pieces(rest)
    second = jnp.concatenate([x, x, y, y, x, z], 1)
    upper[:HALF] = upper1.astype(BF16)
    upper[HALF:] = dot(second, jnp.concatenate([high, middle, high, middle, low, high], 0)).astype(BF16)


def update_kernel(matrix, left, keep, upper, *refs):
    arrived, (out, made, sems) = refs[:-3], refs[-3:]
    has_panel = lax.axis_index("pcol") == 0
    copies = []
    for j in range(matrix.shape[1] // NB):
        cols = slice(j * NB, (j + 1) * NB)

        def compute(cols=cols):
            swaps = arrived[0][:, cols]
            for other in arrived[1:]:
                swaps = swaps + other[:, cols]
            change = dot(left[...], jnp.concatenate([upper[:, cols], swaps], 0))
            kept = matrix[:, cols] * jnp.concatenate([keep[...], keep[...]], 1)
            made[:, cols] = (kept.astype(F32) + change).astype(BF16)

        def as_it_is(cols=cols):
            made[:, cols] = matrix[:, cols]

        if j == 0:
            pl.when(has_panel)(as_it_is)
            pl.when(jnp.logical_not(has_panel))(compute)
        else:
            compute()
        copies.append(pltpu.make_async_copy(made.at[:, cols], out.at[:, cols], sems.at[j]))
        copies[-1].start()
    for copy in copies:
        copy.wait()


SHAPE = jax.ShapeDtypeStruct
WHOLE = pl.BlockSpec(memory_space=pltpu.VMEM)


def params(limit=16):
    return pltpu.CompilerParams(vmem_limit_bytes=limit << 20)


def cost(flops=0, nbytes=0):
    return pl.CostEstimate(flops=flops, bytes_accessed=nbytes, transcendentals=0)


def prepare(height, swaps, mine, received, place):
    return pl.pallas_call(
        functools.partial(prepare_kernel, swaps),
        out_shape=[SHAPE((height, NB + swaps), BF16), SHAPE((height, HALF), BF16)],
        in_specs=[WHOLE] * 3,
        out_specs=[WHOLE] * 2,
        compiler_params=params(),
        name="prepare",
    )(mine, received, place)


def solve(width, block, inverse, gather, parts):
    return pl.pallas_call(
        solve_kernel,
        out_shape=SHAPE((NB, width), BF16),
        in_specs=[WHOLE] * (3 + len(parts)),
        out_specs=WHOLE,
        compiler_params=params(),
        name="solve",
    )(block, inverse, gather, *parts)


def update(matrix, left, keep, upper, arrived):
    return pl.pallas_call(
        update_kernel,
        out_shape=SHAPE(matrix.shape, BF16),
        in_specs=[WHOLE] * (4 + len(arrived)),
        out_specs=pl.BlockSpec(memory_space=pl.ANY),
        scratch_shapes=[
            pltpu.VMEM(matrix.shape, BF16),
            pltpu.SemaphoreType.DMA((matrix.shape[1] // NB,)),
        ],
        compiler_params=params(24),
        name="update",
    )(matrix, left, keep, upper, *arrived)


def spread(value, axes, index, count, stride=1, after_first=None):
    step = count // 2
    while step:
        pairs = [(i * stride, (i + step) * stride) for i in range(0, count, 2 * step)]
        received = lax.ppermute(value, axes, pairs)
        if after_first is not None and step == count // 2:
            received, after_first = lax.optimization_barrier((received, after_first))
        takes = lax.rem(index, 2 * step * stride) == step * stride
        value = jnp.where(takes, received, value)
        step //= 2
    return value if after_first is None else (value, *after_first)


def local(matrix, pivots):
    height, width = matrix.shape
    row_groups, col_groups = lax.axis_size("prow"), lax.axis_size("pcol")
    row_me, col_me = lax.axis_index("prow"), lax.axis_index("pcol")
    outer, inner = grid_of(row_groups)
    cap = round_rows(row_groups)
    smem = pl.BlockSpec(memory_space=pltpu.SMEM)

    rows, source, landing = pl.pallas_call(
        functools.partial(pick_kernel, row_groups, cap),
        out_shape=[SHAPE((cap, width), BF16), SHAPE((1, NB), I32), SHAPE((1, NB), I32)],
        in_specs=[smem, pl.BlockSpec(memory_space=pl.ANY)],
        out_specs=[WHOLE] * 3,
        scratch_shapes=[
            pltpu.VMEM((height, width), BF16),
            pltpu.SMEM((height * row_groups,), I32),
            pltpu.SMEM((1, NB), I32),
            pltpu.SMEM((1, NB), I32),
            pltpu.SemaphoreType.DMA,
            pltpu.SemaphoreType.DMA,
            pltpu.SemaphoreType.DMA((height // NB,)),
        ],
        compiler_params=params(12),
        cost_estimate=cost(2 * 4 * cap * width * height, 20 << 20),
        name="pick",
    )(pivots, matrix)
    gather, place, flag, *gives = pl.pallas_call(
        functools.partial(tables_kernel, row_groups, cap),
        out_shape=[SHAPE((NB, row_groups * cap), BF16), SHAPE((1, HALF), I32), SHAPE((1, HALF), I32)]
        + [SHAPE((outer * cap, width), BF16)] * inner,
        grid=(1,),
        in_specs=[pl.BlockSpec((1, NB), lambda i: (0, 0))] * 2 + [pl.BlockSpec((NB, width), lambda i: (0, 0))],
        out_specs=[WHOLE] * (3 + inner),
        compiler_params=params(12),
        cost_estimate=cost(2 * 4 * cap * width * height, 4 << 20),
        name="tables",
    )(source, landing, matrix)

    both = ("prow", "pcol")
    me = row_me * col_groups + col_me
    block, flag = spread(matrix[:NB, :NB], both, me, row_groups, col_groups, (flag,))
    block = spread(block, "pcol", col_me, col_groups)
    panel = matrix[:, :NB]
    step = col_groups // 2
    while step > 1:
        pairs = [(i, i + step) for i in range(0, col_groups, 2 * step)]
        received = lax.ppermute(panel, "pcol", pairs)
        panel = jnp.where(lax.rem(col_me, 2 * step) == step, received, panel)
        step //= 2
    passed = lax.ppermute(panel, "pcol", [(i, i + 1) for i in range(0, col_groups, 2)])

    def at(o, i):
        return o % outer * inner + i % inner

    everyone = [(o, i) for o in range(outer) for i in range(inner)]
    parts = [rows]
    for step in range(1, outer):
        parts.append(lax.ppermute(rows, "prow", [(at(o, i), at(o + step, i)) for o, i in everyone]))
    parts = [jnp.concatenate(parts, 0)]
    for turn in range(1, inner):
        parts.append(lax.ppermute(parts[0], "prow", [(at(o, i), at(o, i + turn)) for o, i in everyone]))

    held = gives[0]
    for j in range(1, inner):
        held = jnp.where(row_me == j, lax.ppermute(gives[j], "prow", [(0, j)]), held)
    arrived = [jnp.where(row_me < inner, held[:cap], jnp.zeros((), BF16))]
    for step in range(1, outer):
        piece = held[step * cap : (step + 1) * cap]
        arrived.append(lax.ppermute(piece, "prow", [(i, at(step, i)) for i in range(inner)]))

    inverse = pl.pallas_call(
        invert_kernel,
        out_shape=SHAPE((NB, HALF), F32),
        in_specs=[WHOLE],
        out_specs=WHOLE,
        cost_estimate=cost(2 * 60 * NB * NB * NB),
        name="invert",
    )(block)

    left, keep = prepare(height, cap, panel, passed, place)
    upper = solve(width, block, inverse, gather, parts)
    result = update(matrix, left, keep, upper, arrived)

    def again(state):
        picked, place_all = pl.pallas_call(
            functools.partial(pick_all_kernel, row_groups),
            out_shape=[SHAPE((NB, width), BF16), SHAPE((1, NB), I32)],
            in_specs=[WHOLE] * 3,
            out_specs=[WHOLE] * 2,
            compiler_params=params(),
            name="pick_all",
        )(source, landing, matrix)
        top = picked
        for shift in range(1, row_groups):
            top = top + lax.ppermute(picked, "prow", [(i, (i + shift) % row_groups) for i in range(row_groups)])
        same = (iota((NB, NB), 0) == iota((NB, NB), 1)).astype(BF16)
        old_top = spread(matrix[:NB], "prow", row_me, row_groups)
        left_all, keep_all = prepare(height, NB, panel, passed, place_all)
        upper_all = solve(width, block, inverse, same, [top])
        return jnp.zeros((), jnp.bool_), update(matrix, left_all, keep_all, upper_all, [old_top])

    return lax.while_loop(lambda state: state[0], again, (flag[0, 0] > cap, result))[1]


def solution(mesh):
    placed = (P("prow", "pcol"), P())
    return jax.shard_map(
        local, mesh=mesh, in_specs=placed, out_specs=P("prow", "pcol"), check_vma=False
    )
```

time: 213 us -> 69.5 us (0.33)
  the two profiles are of different devices: /device:TPU:6 before, /device:TPU:0 now
where the time goes in v2:
time: 69.5 us; the launch traced here: 69 us
  starting transfers between devices  25.9 us (37%)
  Pallas kernels  23.2 us (33%)
  waiting for transfers between devices  12.3 us (18%)
  local copies, waits for them, and re-layouts  3.8 us (5%)
  other arithmetic  3.14 us (5%)
    ppermute x5, starting transfers between devices, spread(): received = lax.ppermute(value, axes, pairs)  13.3 us
    ppermute x5, waiting for transfers between devices, spread(): received = lax.ppermute(value, axes, pairs)  9.09 us
    pallas_call x1, Pallas kernels, update(): pl.pallas_call(update_kernel, out_shape=SHAPE(matrix.shape, BF16), in_spe...  7.49 us
    pallas_call x1, Pallas kernels, local(): pl.pallas_call(functools.partial(pick_kernel, row_groups, cap), out_shape...  5.21 us
    pallas_call x1, Pallas kernels, local(): pl.pallas_call(invert_kernel, out_shape=SHAPE((NB, HALF), F32), in_specs=...  5.17 us
    ppermute x3, starting transfers between devices, local(): lax.ppermute(piece, 'prow', [(i, at(step, i)) for i in range(inner)])  4.37 us
    ppermute x1, starting transfers between devices, local(): lax.ppermute(panel, 'pcol', [(i, i + 1) for i in range(0, col_groups, 2)])  3.21 us
    pallas_call x1, Pallas kernels, local(): pl.pallas_call(functools.partial(tables_kernel, row_groups, cap), out_sha...  2.19 us
  transfers between devices with their start and end apart: 15, of which 6 were waited for; matrix products, arithmetic and copies ran while one was open for 8% of the time, Pallas kernels for 23%

profile of v2, /device:TPU:0, one launch (start us, length us, event | category | flops | bytes accessed | tf_op | source)
XLA Modules:
  0.0 69.0 jit_solution(4832832308836807827)
XLA Ops:
  0.0 0.9 %slice.24 = bf16[256,256]{1,0:T(8,128)(2,1)S(1)} slice(bf16[1792,1792]{1,0:T(8,128)(2,1)} %matrix.3), slice={[0:256], [0:256]} | slice | bytes 262144 | tf_op jit(solution)/shard_map/slice | solution.py:354
  0.9 5.9 %collective-permute-start.10 = (bf16[256,256]{1,0:T(8,128)(2,1)S(1)}, bf16[256,256]{1,0:T(8,128)(2,1)S(1)}, u32[]{:S(2)}, u32[]{:S(2)}) collective-permute-start(bf16[256,256]{1,0:T(8,128)(2,1)S(1)} %slice.24), channel_id=1, source_target_pairs={{0,16}} | collective-permute-start | bytes 393224 | tf_op jit(solution)/shard_map/ppermute | solution.py:305
  6.9 0.0 copy-start
  6.9 0.7 copy-done
  7.6 5.2 %pick.1 = (bf16[48,1792]{1,0:T(8,128)(2,1)S(1)}, s32[1,256]{1,0:T(1,128)S(1)}, s32[1,256]{1,0:T(1,128)S(1)}) custom-call(s32[256]{0:T(256)S(1)} %copy-done, bf16[1792,1792]{1,0:T(8,128)(2,1)} %matrix.3), custom_call_target="tpu_custom_call" | custom-call | flops 1233125376 | bytes 20971520 | tf_op jit(solution)/shard_map/pick/pallas_call | solution.py:322
  12.8 0.1 collective-permute-start.19
  12.8 0.1 collective-permute-start.18
  12.9 1.9 %collective-permute-start.17 = (bf16[48,1792]{1,0:T(8,128)(2,1)S(1)}, bf16[48,1792]{1,0:T(8,128)(2,1)S(1)}, u32[]{:S(2)}, u32[]{:S(2)}) collective-permute-start(bf16[48,1792]{1,0:T(8,128)(2,1)S(1)} %get-tuple-element.80), channel_id=1, source_target_pairs={{0,8},{4,12},{8,16},{12,20},{16,24},{20,28},{24,0},{28,4},{1,9},{5... | collective-permute-start | bytes 516104 | tf_op jit(solution)/shard_map/ppermute | solution.py:371
  14.9 2.2 %slice.26 = bf16[1792,256]{1,0:T(8,128)(2,1)} slice(bf16[1792,1792]{1,0:T(8,128)(2,1)} %matrix.3), slice={[0:1792], [0:256]} | slice | bytes 1835008 | tf_op jit(solution)/shard_map/slice | solution.py:356
  17.0 2.2 %tables.1 = (bf16[256,384]{1,0:T(8,128)(2,1)S(1)}, s32[1,128]{1,0:T(1,128)S(1)}, s32[1,128]{1,0:T(1,128)S(1)}, bf16[192,1792]{1,0:T(8,128)(2,1)S(1)}, bf16[192,1792]{1,0:T(8,128)(2,1)S(1)}) custom-call(s32[1,256]{1,0:T(1,128)S(1)} %get-tuple-element.120.source, s32[1,256]{1,0:T(1,128)S(1)} %get-tuple-element.121.landing, bf16[1792,1792]{1,0:T(8,128)(2,1)} %matrix.3), custom_call_target="tpu_custom_call" | custom-call | flops 1233125376 | bytes 4194304 | tf_op jit(solution)/shard_map/tables/pallas_call | solution.py:340
  19.2 0.0 collective-permute-done.10
  19.2 0.9 %broadcast_select_fusion.5 = bf16[256,256]{1,0:T(8,128)(2,1)S(1)} fusion(bf16[256,256]{1,0:T(8,128)(2,1)S(1)} %collective-permute-done.10, pred[]{:T(512)S(6)} %eq.35, bf16[1792,1792]{1,0:T(8,128)(2,1)} %matrix.3), kind=kLoop, calls=%fused_computation.9 | loop fusion | flops 65536 | bytes 393217 | tf_op jit(solution)/shard_map/jit(_where)/select_n | solution.py:309
  20.2 3.5 %collective-permute-start.13 = (bf16[256,256]{1,0:T(8,128)(2,1)S(1)}, bf16[256,256]{1,0:T(8,128)(2,1)S(1)}, u32[]{:S(2)}, u32[]{:S(2)}) collective-permute-start(bf16[256,256]{1,0:T(8,128)(2,1)S(1)} %broadcast_select_fusion.5), channel_id=1, source_target_pairs={{0,8},{16,24}} | collective-permute-start | bytes 393224 | tf_op jit(solution)/shard_map/ppermute | solution.py:305
  23.7 1.3 %collective-permute-start.11 = (bf16[1792,256]{1,0:T(8,128)(2,1)}, bf16[1792,256]{1,0:T(8,128)(2,1)S(1)}, u32[]{:S(2)}, u32[]{:S(2)}) collective-permute-start(bf16[1792,256]{1,0:T(8,128)(2,1)} %slice.26), channel_id=1, source_target_pairs={{0,2},{4,6},{8,10},{12,14},{16,18},{20,22},{24,26},{28,30}} | collective-permute-start | bytes 2752520 | tf_op jit(solution)/shard_map/ppermute | solution.py:360
  25.0 1.1 %collective-permute-done.13 = bf16[256,256]{1,0:T(8,128)(2,1)S(1)} collective-permute-done((bf16[256,256]{1,0:T(8,128)(2,1)S(1)}, bf16[256,256]{1,0:T(8,128)(2,1)S(1)}, u32[]{:S(2)}, u32[]{:S(2)}) %collective-permute-start.13) | collective-permute-done | bytes 131104 | tf_op jit(solution)/shard_map/ppermute | solution.py:305
  26.1 1.3 %collective-permute-start.14 = (bf16[256,256]{1,0:T(8,128)(2,1)S(1)}, bf16[256,256]{1,0:T(8,128)(2,1)S(1)}, u32[]{:S(2)}, u32[]{:S(2)}) collective-permute-start(bf16[256,256]{1,0:T(8,128)(2,1)S(1)} %broadcast_select_fusion.6), channel_id=1, source_target_pairs={{0,4},{8,12},{16,20},{24,28}} | collective-permute-start | bytes 393224 | tf_op jit(solution)/shard_map/ppermute | solution.py:305
  27.4 0.0 collective-permute-done.17
  27.5 1.3 %collective-permute-start.21 = (bf16[192,1792]{1,0:T(8,128)(2,1)S(1)}, bf16[192,1792]{1,0:T(8,128)(2,1)S(1)}, u32[]{:S(2)}, u32[]{:S(2)}) collective-permute-start(bf16[192,1792]{1,0:T(8,128)(2,1)S(1)} %get-tuple-element.81), channel_id=1, source_target_pairs={{0,4},{1,5},{2,6},{3,7}} | collective-permute-start | bytes 2064392 | tf_op jit(solution)/shard_map/ppermute | solution.py:378
  28.8 2.5 %collective-permute-done.14 = bf16[256,256]{1,0:T(8,128)(2,1)S(1)} collective-permute-done((bf16[256,256]{1,0:T(8,128)(2,1)S(1)}, bf16[256,256]{1,0:T(8,128)(2,1)S(1)}, u32[]{:S(2)}, u32[]{:S(2)}) %collective-permute-start.14) | collective-permute-done | bytes 131104 | tf_op jit(solution)/shard_map/ppermute | solution.py:305
  31.4 1.3 %collective-permute-start.15 = (bf16[256,256]{1,0:T(8,128)(2,1)S(1)}, bf16[256,256]{1,0:T(8,128)(2,1)S(1)}, u32[]{:S(2)}, u32[]{:S(2)}) collective-permute-start(bf16[256,256]{1,0:T(8,128)(2,1)S(1)} %broadcast_select_fusion.7), channel_id=1, source_target_pairs={{0,2},{4,6},{8,10},{12,14},{16,18},{20,22},{24,26},{28,30}} | collective-permute-start | bytes 393224 | tf_op jit(solution)/shard_map/ppermute | solution.py:305
  32.7 0.0 collective-permute-done.18
  32.7 4.8 %collective-permute-done.15 = bf16[256,256]{1,0:T(8,128)(2,1)S(1)} collective-permute-done((bf16[256,256]{1,0:T(8,128)(2,1)S(1)}, bf16[256,256]{1,0:T(8,128)(2,1)S(1)}, u32[]{:S(2)}, u32[]{:S(2)}) %collective-permute-start.15) | collective-permute-done | bytes 131104 | tf_op jit(solution)/shard_map/ppermute | solution.py:305
  37.5 1.3 %collective-permute-start.16 = (bf16[256,256]{1,0:T(8,128)(2,1)S(1)}, bf16[256,256]{1,0:T(8,128)(2,1)S(1)}, u32[]{:S(2)}, u32[]{:S(2)}) collective-permute-start(bf16[256,256]{1,0:T(8,128)(2,1)S(1)} %broadcast_select_fusion.8), channel_id=1, source_target_pairs={{0,1},{2,3},{4,5},{6,7},{8,9},{10,11},{12,13},{14,15},{16,17},{18,... | collective-permute-start | bytes 393224 | tf_op jit(solution)/shard_map/ppermute | solution.py:305
  38.8 0.0 collective-permute-done.19
  38.8 0.2 collective-permute-start.20
  39.1 0.7 collective-permute-done.16
  39.8 0.0 collective-permute-done.11
  39.8 1.3 %broadcast_select_fusion.3.mine = bf16[1792,256]{1,0:T(8,128)(2,1)S(1)} fusion(bf16[1792,256]{1,0:T(8,128)(2,1)S(1)} %collective-permute-done.11, pred[]{:T(512)S(6)} %eq.31, bf16[1792,1792]{1,0:T(8,128)(2,1)} %matrix.3), kind=kLoop, calls=%fused_computation.6 | loop fusion | flops 458752 | bytes 2752513 | tf_op jit(solution)/shard_map/jit(_where)/select_n | solution.py:361
  41.1 3.2 %collective-permute-start.12 = (bf16[1792,256]{1,0:T(8,128)(2,1)S(1)}, bf16[1792,256]{1,0:T(8,128)(2,1)}, u32[]{:S(2)}, u32[]{:S(2)}) collective-permute-start(bf16[1792,256]{1,0:T(8,128)(2,1)S(1)} %broadcast_select_fusion.3.mine), channel_id=1, source_target_pairs={{0,1},{2,3},{4,5},{6,7},{8,9},{10,11},{12,13},{14,15},{16,17},{18,... | collective-permute-start | bytes 2752520 | tf_op jit(solution)/shard_map/ppermute | solution.py:363
  44.3 1.8 %collective-permute-done.21 = bf16[192,1792]{1,0:T(8,128)(2,1)S(1)} collective-permute-done((bf16[192,1792]{1,0:T(8,128)(2,1)S(1)}, bf16[192,1792]{1,0:T(8,128)(2,1)S(1)}, u32[]{:S(2)}, u32[]{:S(2)}) %collective-permute-start.21) | collective-permute-done | bytes 688160 | tf_op jit(solution)/shard_map/ppermute | solution.py:378
  46.1 0.1 broadcast_select_fusion.4
  46.2 0.8 %fusion.1 = (bf16[48,1792]{1,0:T(8,128)(2,1)}, bf16[48,1792]{1,0:T(8,128)(2,1)}, bf16[48,1792]{1,0:T(8,128)(2,1)}, bf16[48,1792]{1,0:T(8,128)(2,1)S(1)}) fusion(bf16[192,1792]{1,0:T(8,128)(2,1)S(1)} %broadcast_select_fusion.4, pred[]{:T(512)S(6)} %lt.3), kind=kLoop, calls=%fused_computation.18 | loop fusion | flops 86016 | bytes 1376257 | tf_op jit(solution)/shard_map/slice | solution.py:381
  47.0 1.8 %collective-permute-start.24 = (bf16[48,1792]{1,0:T(8,128)(2,1)}, bf16[48,1792]{1,0:T(8,128)(2,1)S(1)}, u32[]{:S(2)}, u32[]{:S(2)}) collective-permute-start(bf16[48,1792]{1,0:T(8,128)(2,1)} %get-tuple-element.104), channel_id=1, source_target_pairs={{0,24},{4,28},{1,25},{5,29},{2,26},{6,30},{3,27},{7,31}} | collective-permute-start | bytes 516104 | tf_op jit(solution)/shard_map/ppermute | solution.py:382
  48.8 1.3 %collective-permute-start.23 = (bf16[48,1792]{1,0:T(8,128)(2,1)}, bf16[48,1792]{1,0:T(8,128)(2,1)S(1)}, u32[]{:S(2)}, u32[]{:S(2)}) collective-permute-start(bf16[48,1792]{1,0:T(8,128)(2,1)} %get-tuple-element.105), channel_id=1, source_target_pairs={{0,16},{4,20},{1,17},{5,21},{2,18},{6,22},{3,19},{7,23}} | collective-permute-start | bytes 516104 | tf_op jit(solution)/shard_map/ppermute | solution.py:382
  50.1 1.3 %collective-permute-start.22 = (bf16[48,1792]{1,0:T(8,128)(2,1)}, bf16[48,1792]{1,0:T(8,128)(2,1)S(1)}, u32[]{:S(2)}, u32[]{:S(2)}) collective-permute-start(bf16[48,1792]{1,0:T(8,128)(2,1)} %get-tuple-element.106), channel_id=1, source_target_pairs={{0,8},{4,12},{1,9},{5,13},{2,10},{6,14},{3,11},{7,15}} | collective-permute-start | bytes 516104 | tf_op jit(solution)/shard_map/ppermute | solution.py:382
  51.4 5.2 %invert.1.inverse = f32[256,128]{1,0:T(8,128)S(1)} custom-call(bf16[256,256]{1,0:T(8,128)(2,1)S(1)} %broadcast_select_fusion.9.block), custom_call_target="tpu_custom_call" | custom-call | flops 2013265920 | tf_op jit(solution)/shard_map/invert/pallas_call | solution.py:384
  56.5 1.4 %collective-permute-done.20.refs_1_ = bf16[192,1792]{1,0:T(8,128)(2,1)S(1)} collective-permute-done((bf16[192,1792]{1,0:T(8,128)(2,1)S(1)}, bf16[192,1792]{1,0:T(8,128)(2,1)S(1)}, u32[]{:S(2)}, u32[]{:S(2)}) %collective-permute-start.20) | collective-permute-done | bytes 688160 | tf_op jit(solution)/shard_map/ppermute | solution.py:374
  58.0 1.5 %solve.3.upper = bf16[256,1792]{1,0:T(8,128)(2,1)S(1)} custom-call(bf16[256,256]{1,0:T(8,128)(2,1)S(1)} %broadcast_select_fusion.9.block, f32[256,128]{1,0:T(8,128)S(1)} %invert.1.inverse, bf16[256,384]{1,0:T(8,128)(2,1)S(1)} %get-tuple-element.79.gather, bf16[192,1792]{1,0:T(8,128)(2,1)S(1)} %constant_dynamic-update-slice_fusion.refs_0_, ...), custom_call_target="tpu_custom_call" | custom-call | tf_op jit(solution)/shard_map/solve/pallas_call | solution.py:276
  59.5 0.0 collective-permute-done.12.received
  59.5 1.6 %prepare.3 = (bf16[1792,304]{1,0:T(8,128)(2,1)S(1)}, bf16[1792,128]{1,0:T(8,128)(2,1)S(1)}) custom-call(bf16[1792,256]{1,0:T(8,128)(2,1)S(1)} %broadcast_select_fusion.3.mine, bf16[1792,256]{1,0:T(8,128)(2,1)} %collective-permute-done.12.received, s32[1,128]{1,0:T(1,128)S(1)} %get-tuple-element.75.place), custom_call_target="tpu_custom_call" | custom-call | tf_op jit(solution)/shard_map/prepare/pallas_call | solution.py:265
  61.1 0.0 collective-permute-done.24.refs_3_
  61.1 0.0 collective-permute-done.23.refs_2_
  61.1 0.0 collective-permute-done.22.refs_1_
  61.1 7.5 %update.3 = bf16[1792,1792]{1,0:T(8,128)(2,1)} custom-call(bf16[1792,1792]{1,0:T(8,128)(2,1)} %matrix.3, bf16[1792,304]{1,0:T(8,128)(2,1)S(1)} %get-tuple-element.76.left, bf16[1792,128]{1,0:T(8,128)(2,1)S(1)} %get-tuple-element.77.keep, bf16[256,1792]{1,0:T(8,128)(2,1)S(1)} %solve.3.upper, bf16[48,1792]{1,0:T(8,128)(2,1)S(1)} %get-tuple-element.107.refs_0_, ...), custom_call_target="tpu_custom_call" | custom-call | tf_op jit(solution)/shard_map/update/pallas_call | solution.py:287
  68.6 0.2 while.9
  (8 shorter events, 0.1 us)
Async XLA Ops:
  0.9 18.3 %collective-permute-start.10 = (bf16[256,256]{1,0:T(8,128)(2,1)S(1)}, bf16[256,256]{1,0:T(8,128)(2,1)S(1)}, u32[]{:S(2)}, u32[]{:S(2)}) collective-permute-start(bf16[256,256]{1,0:T(8,128)(2,1)S(1)} %slice.24), channel_id=1, source_target_pairs={{0,16}} | collective-permute-start | bytes 393224 | tf_op jit(solution)/shard_map/ppermute | solution.py:305
  6.9 0.7 copy-start
  12.8 26.0 %collective-permute-start.19 = (bf16[48,1792]{1,0:T(8,128)(2,1)S(1)}, bf16[48,1792]{1,0:T(8,128)(2,1)S(1)}, u32[]{:S(2)}, u32[]{:S(2)}) collective-permute-start(bf16[48,1792]{1,0:T(8,128)(2,1)S(1)} %get-tuple-element.80), channel_id=1, source_target_pairs={{0,24},{4,28},{8,0},{12,4},{16,8},{20,12},{24,16},{28,20},{1,25},{... | collective-permute-start | bytes 516104 | tf_op jit(solution)/shard_map/ppermute | solution.py:371
  12.8 19.8 %collective-permute-start.18 = (bf16[48,1792]{1,0:T(8,128)(2,1)S(1)}, bf16[48,1792]{1,0:T(8,128)(2,1)S(1)}, u32[]{:S(2)}, u32[]{:S(2)}) collective-permute-start(bf16[48,1792]{1,0:T(8,128)(2,1)S(1)} %get-tuple-element.80), channel_id=1, source_target_pairs={{0,16},{4,20},{8,24},{12,28},{16,0},{20,4},{24,8},{28,12},{1,17},{... | collective-permute-start | bytes 516104 | tf_op jit(solution)/shard_map/ppermute | solution.py:371
  12.9 14.5 %collective-permute-start.17 = (bf16[48,1792]{1,0:T(8,128)(2,1)S(1)}, bf16[48,1792]{1,0:T(8,128)(2,1)S(1)}, u32[]{:S(2)}, u32[]{:S(2)}) collective-permute-start(bf16[48,1792]{1,0:T(8,128)(2,1)S(1)} %get-tuple-element.80), channel_id=1, source_target_pairs={{0,8},{4,12},{8,16},{12,20},{16,24},{20,28},{24,0},{28,4},{1,9},{5... | collective-permute-start | bytes 516104 | tf_op jit(solution)/shard_map/ppermute | solution.py:371
  20.2 6.0 %collective-permute-start.13 = (bf16[256,256]{1,0:T(8,128)(2,1)S(1)}, bf16[256,256]{1,0:T(8,128)(2,1)S(1)}, u32[]{:S(2)}, u32[]{:S(2)}) collective-permute-start(bf16[256,256]{1,0:T(8,128)(2,1)S(1)} %broadcast_select_fusion.5), channel_id=1, source_target_pairs={{0,8},{16,24}} | collective-permute-start | bytes 393224 | tf_op jit(solution)/shard_map/ppermute | solution.py:305
  23.7 16.1 %collective-permute-start.11 = (bf16[1792,256]{1,0:T(8,128)(2,1)}, bf16[1792,256]{1,0:T(8,128)(2,1)S(1)}, u32[]{:S(2)}, u32[]{:S(2)}) collective-permute-start(bf16[1792,256]{1,0:T(8,128)(2,1)} %slice.26), channel_id=1, source_target_pairs={{0,2},{4,6},{8,10},{12,14},{16,18},{20,22},{24,26},{28,30}} | collective-permute-start | bytes 2752520 | tf_op jit(solution)/shard_map/ppermute | solution.py:360
  26.1 5.2 %collective-permute-start.14 = (bf16[256,256]{1,0:T(8,128)(2,1)S(1)}, bf16[256,256]{1,0:T(8,128)(2,1)S(1)}, u32[]{:S(2)}, u32[]{:S(2)}) collective-permute-start(bf16[256,256]{1,0:T(8,128)(2,1)S(1)} %broadcast_select_fusion.6), channel_id=1, source_target_pairs={{0,4},{8,12},{16,20},{24,28}} | collective-permute-start | bytes 393224 | tf_op jit(solution)/shard_map/ppermute | solution.py:305
  27.5 18.6 %collective-permute-start.21 = (bf16[192,1792]{1,0:T(8,128)(2,1)S(1)}, bf16[192,1792]{1,0:T(8,128)(2,1)S(1)}, u32[]{:S(2)}, u32[]{:S(2)}) collective-permute-start(bf16[192,1792]{1,0:T(8,128)(2,1)S(1)} %get-tuple-element.81), channel_id=1, source_target_pairs={{0,4},{1,5},{2,6},{3,7}} | collective-permute-start | bytes 2064392 | tf_op jit(solution)/shard_map/ppermute | solution.py:378
  31.4 6.1 %collective-permute-start.15 = (bf16[256,256]{1,0:T(8,128)(2,1)S(1)}, bf16[256,256]{1,0:T(8,128)(2,1)S(1)}, u32[]{:S(2)}, u32[]{:S(2)}) collective-permute-start(bf16[256,256]{1,0:T(8,128)(2,1)S(1)} %broadcast_select_fusion.7), channel_id=1, source_target_pairs={{0,2},{4,6},{8,10},{12,14},{16,18},{20,22},{24,26},{28,30}} | collective-permute-start | bytes 393224 | tf_op jit(solution)/shard_map/ppermute | solution.py:305
  37.5 2.3 %collective-permute-start.16 = (bf16[256,256]{1,0:T(8,128)(2,1)S(1)}, bf16[256,256]{1,0:T(8,128)(2,1)S(1)}, u32[]{:S(2)}, u32[]{:S(2)}) collective-permute-start(bf16[256,256]{1,0:T(8,128)(2,1)S(1)} %broadcast_select_fusion.8), channel_id=1, source_target_pairs={{0,1},{2,3},{4,5},{6,7},{8,9},{10,11},{12,13},{14,15},{16,17},{18,... | collective-permute-start | bytes 393224 | tf_op jit(solution)/shard_map/ppermute | solution.py:305
  38.8 19.1 %collective-permute-start.20 = (bf16[192,1792]{1,0:T(8,128)(2,1)S(1)}, bf16[192,1792]{1,0:T(8,128)(2,1)S(1)}, u32[]{:S(2)}, u32[]{:S(2)}) collective-permute-start(bf16[192,1792]{1,0:T(8,128)(2,1)S(1)} %constant_dynamic-update-slice_fusion.refs_0_), channel_id=1, source_target_pairs={{0,4},{4,0},{8,12},{12,8},{16,20},{20,16},{24,28},{28,24},{1,5},{5... | collective-permute-start | bytes 2064392 | tf_op jit(solution)/shard_map/ppermute | solution.py:374
  41.1 18.4 %collective-permute-start.12 = (bf16[1792,256]{1,0:T(8,128)(2,1)S(1)}, bf16[1792,256]{1,0:T(8,128)(2,1)}, u32[]{:S(2)}, u32[]{:S(2)}) collective-permute-start(bf16[1792,256]{1,0:T(8,128)(2,1)S(1)} %broadcast_select_fusion.3.mine), channel_id=1, source_target_pairs={{0,1},{2,3},{4,5},{6,7},{8,9},{10,11},{12,13},{14,15},{16,17},{18,... | collective-permute-start | bytes 2752520 | tf_op jit(solution)/shard_map/ppermute | solution.py:363
  47.0 14.1 %collective-permute-start.24 = (bf16[48,1792]{1,0:T(8,128)(2,1)}, bf16[48,1792]{1,0:T(8,128)(2,1)S(1)}, u32[]{:S(2)}, u32[]{:S(2)}) collective-permute-start(bf16[48,1792]{1,0:T(8,128)(2,1)} %get-tuple-element.104), channel_id=1, source_target_pairs={{0,24},{4,28},{1,25},{5,29},{2,26},{6,30},{3,27},{7,31}} | collective-permute-start | bytes 516104 | tf_op jit(solution)/shard_map/ppermute | solution.py:382
  48.8 12.3 %collective-permute-start.23 = (bf16[48,1792]{1,0:T(8,128)(2,1)}, bf16[48,1792]{1,0:T(8,128)(2,1)S(1)}, u32[]{:S(2)}, u32[]{:S(2)}) collective-permute-start(bf16[48,1792]{1,0:T(8,128)(2,1)} %get-tuple-element.105), channel_id=1, source_target_pairs={{0,16},{4,20},{1,17},{5,21},{2,18},{6,22},{3,19},{7,23}} | collective-permute-start | bytes 516104 | tf_op jit(solution)/shard_map/ppermute | solution.py:382
  50.1 11.1 %collective-permute-start.22 = (bf16[48,1792]{1,0:T(8,128)(2,1)}, bf16[48,1792]{1,0:T(8,128)(2,1)S(1)}, u32[]{:S(2)}, u32[]{:S(2)}) collective-permute-start(bf16[48,1792]{1,0:T(8,128)(2,1)} %get-tuple-element.106), channel_id=1, source_target_pairs={{0,8},{4,12},{1,9},{5,13},{2,10},{6,14},{3,11},{7,15}} | collective-permute-start | bytes 516104 | tf_op jit(solution)/shard_map/ppermute | solution.py:382

commit v3 on v2

v3 whole, which is shorter than its diff:
```python
import functools

import jax
import jax.numpy as jnp
from jax import lax
from jax.experimental import pallas as pl
from jax.experimental.pallas import tpu as pltpu
from jax.sharding import PartitionSpec as P

NB = 256
HALF = 128
BF16 = jnp.bfloat16
F32 = jnp.float32
I32 = jnp.int32


def grid_of(row_groups):
    outer = 4 if row_groups % 4 == 0 else row_groups
    return outer, row_groups // outer


def round_rows(row_groups):
    share = -(-3 * NB // (2 * row_groups))
    return min(NB, -(-share // 16) * 16)


def iota(shape, dim):
    return lax.broadcasted_iota(I32, shape, dim)


def dot(a, b):
    return jnp.dot(a, b, preferred_element_type=F32)


def block_owner(global_row, row_groups):
    block = lax.shift_right_logical(global_row, 8)
    if row_groups & (row_groups - 1) == 0:
        return block & (row_groups - 1), lax.shift_right_logical(block, row_groups.bit_length() - 1)
    return lax.rem(block, row_groups), lax.div(block, row_groups)


def place_of(source, row_groups):
    owner, block = block_owner(source, row_groups)
    return owner, block * NB + (source & (NB - 1))


def follow_swaps(pivots, anchor, source, landing, source_out, landing_out, source_sem, landing_sem):
    def start(k, _):
        anchor[pivots[k]] = pivots[k]
        return 0

    def swap(k, _):
        target = pivots[k]
        at_column, at_target = anchor[k], anchor[target]
        anchor[k] = at_target
        anchor[target] = at_column
        return 0

    def write(k, _):
        row = anchor[k]
        source[0, k] = row
        landing[0, k] = jnp.where(row >= NB, anchor[row], -1)
        return 0

    lax.fori_loop(0, NB, start, 0, unroll=16)
    for k in range(NB):
        anchor[k] = k
    lax.fori_loop(0, NB, swap, 0, unroll=16)
    lax.fori_loop(0, NB, write, 0, unroll=16)
    one = pltpu.make_async_copy(source, source_out, source_sem)
    two = pltpu.make_async_copy(landing, landing_out, landing_sem)
    one.start()
    two.start()
    one.wait()
    two.wait()


def as_column(row):
    n = row.shape[1]
    wide = jnp.broadcast_to(row, (n, n))
    on_diagonal = iota((n, n), 0) == iota((n, n), 1)
    return jnp.sum(jnp.where(on_diagonal, wide, 0), axis=1, keepdims=True)


def pick_kernel(row_groups, cap, pivots, matrix, rows, source_out, landing_out, *refs):
    outer, inner = grid_of(row_groups)
    gives, scratch = refs[:inner], refs[inner:]
    held, anchor, source, landing, source_sem, landing_sem, sems = scratch
    height = matrix.shape[0]
    loads = []
    for i in range(height // NB):
        part = pl.ds(i * NB, NB)
        loads.append(pltpu.make_async_copy(matrix.at[part], held.at[part], sems.at[i]))
        loads[-1].start()
    follow_swaps(pivots, anchor, source, landing, source_out, landing_out, source_sem, landing_sem)
    me = lax.axis_index("prow")
    owner, local = place_of(source_out[...], row_groups)
    slot, _ = slots_of(owner, row_groups)
    hit = (slot == iota((cap, NB), 0)) & (owner == me)
    my_rows = jnp.max(jnp.where(hit, local, -1), axis=1, keepdims=True)
    for load in loads:
        load.wait()
    chosen = (my_rows == iota((cap, height), 1)).astype(BF16)
    rows[...] = dot(chosen, held[...]).astype(BF16)
    land = landing_out[...]
    code = jnp.where(slot < cap, owner * cap + slot, -1)
    for j in range(inner):
        wanted = []
        for z in range(outer):
            hit = code == iota((cap, NB), 0) + (z * inner + j) * cap
            wanted.append(jnp.max(jnp.where(hit, land, -1), axis=1, keepdims=True))
        chosen_top = (jnp.concatenate(wanted, 0) == iota((outer * cap, NB), 1)).astype(BF16)
        gives[j][...] = dot(chosen_top, held[:NB]).astype(BF16)


def slots_of(owner, row_groups):
    is_owner = (iota((row_groups, NB), 0) == owner).astype(BF16)
    upto = (iota((NB, NB), 0) <= iota((NB, NB), 1)).astype(BF16)
    ranks = dot(is_owner, upto)
    slot = jnp.sum(jnp.where(is_owner > 0, ranks, 0.0), axis=0, keepdims=True).astype(I32) - 1
    return slot, jnp.max(ranks, axis=(0, 1), keepdims=True).astype(I32)


def tables_kernel(row_groups, cap, source, landing, gather, place, flag):
    outer, inner = grid_of(row_groups)
    me = lax.axis_index("prow")
    land = landing[...]
    owner, local = place_of(source[...], row_groups)
    slot, most = slots_of(owner, row_groups)
    flag[...] = jnp.broadcast_to(most, flag.shape)
    code = jnp.where(slot < cap, owner * cap + slot, -1)
    code_column = as_column(code)
    lands_column = as_column(jnp.where(land >= 0, local, -1))
    mine = code_column - me * cap == iota((NB, HALF), 1)
    mine = mine & (iota((NB, HALF), 1) < cap)
    place[...] = jnp.max(jnp.where(mine, lands_column, -1), axis=0, keepdims=True)
    my_outer, my_inner = me // inner, me % inner
    for turn in range(inner):
        for step in range(outer):
            from_outer = lax.rem(my_outer - step + outer, outer)
            from_inner = lax.rem(my_inner - turn + inner, inner)
            first = (from_outer * inner + from_inner) * cap
            at = (turn * outer + step) * cap
            gather[:, at : at + cap] = (code_column == iota((NB, cap), 1) + first).astype(BF16)


def turn_kernel(row_groups, cap, *refs):
    outer, inner = grid_of(row_groups)
    parts, own, bundles = refs[:outer], refs[outer], refs[outer + 1 : outer + inner]
    gathered, *sent = refs[outer + inner :]
    me = lax.axis_index("prow")
    for i, part in enumerate(parts):
        gathered[i * cap : (i + 1) * cap] = part[...]

    def pass_on(bundle):
        for i, piece in enumerate(sent):
            piece[...] = bundle[i * cap : (i + 1) * cap]

    pl.when(me == 0)(lambda: pass_on(own))
    for j, bundle in enumerate(bundles):
        pl.when(me == j + 1)(functools.partial(pass_on, bundle))

    @pl.when(me >= inner)
    def _():
        for piece in sent:
            piece[...] = jnp.zeros(piece.shape, BF16)


def pick_all_kernel(row_groups, pivots, matrix, rows, place, *scratch):
    source, landing, anchor, source_in, landing_in, source_sem, landing_sem = scratch
    follow_swaps(pivots, anchor, source_in, landing_in, source, landing, source_sem, landing_sem)
    owner, local = place_of(source[...], row_groups)
    mine = owner == lax.axis_index("prow")
    wanted = as_column(jnp.where(mine, local, -1))
    chosen = (wanted == iota((NB, matrix.shape[0]), 1)).astype(BF16)
    rows[...] = dot(chosen, matrix[...]).astype(BF16)
    from_top = as_column(jnp.where(mine, landing[...], -1)) == iota((NB, NB), 1)
    place[...] = jnp.max(jnp.where(from_top, wanted, -1), axis=0, keepdims=True)


def pieces(x):
    high = x.astype(BF16)
    rest = x - high.astype(F32)
    middle = rest.astype(BF16)
    return high, middle, (rest - middle.astype(F32)).astype(BF16)


def invert_kernel(block, inverse):
    rows, cols = iota((HALF, HALF), 0), iota((HALF, HALF), 1)
    apart = rows ^ cols
    none = jnp.zeros((), BF16)
    halves = [slice(0, HALF), slice(HALF, NB)]
    lowers = [jnp.where(rows > cols, block[part, part], none) for part in halves]

    def corner(lower, size):
        return jnp.where((apart >= size) & (apart < 2 * size), lower, none)

    found = [jnp.where(rows == cols, 1.0, 0.0) - corner(lower, 1).astype(F32) for lower in lowers]
    size = 2
    while size < HALF:
        for i, lower in enumerate(lowers):
            x, edge = found[i], corner(lower, size)
            high, middle, low = pieces(x)
            first, second, third = pieces((dot(edge, low) + dot(edge, middle)) + dot(edge, high))
            small = (dot(high, third) + dot(low, first)) + dot(middle, second)
            found[i] = x - ((small + (dot(high, second) + dot(middle, first))) + dot(high, first))
        size *= 2
    for part, x in zip(halves, found):
        inverse[part] = x


def finish_kernel(n_parts, swaps, *refs):
    matrix, mine, passed, place, block, inverse, gather = refs[:7]
    parts, arrived = refs[7 : 7 + n_parts], refs[7 + n_parts : -7]
    out, made, left, keep, upper, load_sems, store_sems = refs[-7:]
    row_me, col_me = lax.axis_index("prow"), lax.axis_index("pcol")
    height, width = made.shape
    loads = []
    for i in range(height // NB):
        part = pl.ds(i * NB, NB)
        loads.append(pltpu.make_async_copy(matrix.at[part], made.at[part], load_sems.at[i]))
        loads[-1].start()

    @pl.when(col_me % 2 == 0)
    def _():
        left[:, :NB] = -mine[:height]

    @pl.when(col_me % 2 == 1)
    def _():
        left[:, :NB] = -passed[:height]

    hit = (iota((height, place.shape[1]), 0) == place[...]).astype(BF16)
    left[:, NB:] = hit[:, :swaps]
    gone = dot(hit, jnp.ones((place.shape[1], HALF), BF16))
    keep[...] = (1.0 - gone).astype(BF16)

    @pl.when(row_me == 0)
    def _():
        keep[:NB] = jnp.zeros((NB, HALF), BF16)
        left[:NB, :NB] = (iota((NB, NB), 0) == iota((NB, NB), 1)).astype(BF16)
        left[:NB, NB:] = jnp.zeros((NB, swaps), BF16)

    rows = jnp.concatenate([part[...] for part in parts], 0)
    top = dot(gather[...], rows)
    top1 = top[:HALF].astype(BF16)
    first = jnp.concatenate(pieces(inverse[:HALF]), 1)
    upper1 = dot(first, jnp.concatenate([top1] * 3, 0))
    edge = block[HALF:, :HALF]
    edges = jnp.concatenate([edge, edge, edge], 1)
    rest = top[HALF:] - dot(edges, jnp.concatenate(pieces(upper1), 0))
    x, y, z = pieces(inverse[HALF:])
    high, middle, low = pieces(rest)
    second = jnp.concatenate([x, x, y, y, x, z], 1)
    upper[:HALF] = upper1.astype(BF16)
    upper[HALF:NB] = dot(second, jnp.concatenate([high, middle, high, middle, low, high], 0)).astype(BF16)
    moved = arrived[0][...]
    for other in arrived[1:]:
        moved = moved + other[...]
    upper[NB:] = moved

    for load in loads:
        load.wait()
    stores = []
    for j in range(width // NB):
        cols = slice(j * NB, (j + 1) * NB)

        def compute(cols=cols):
            change = dot(left[...], upper[:, cols])
            kept = made[:, cols] * jnp.concatenate([keep[...], keep[...]], 1)
            made[:, cols] = (kept.astype(F32) + change).astype(BF16)

        if j == 0:
            pl.when(col_me != 0)(compute)
        else:
            compute()
        stores.append(pltpu.make_async_copy(made.at[:, cols], out.at[:, cols], store_sems.at[j]))
        stores[-1].start()
    for store in stores:
        store.wait()


SHAPE = jax.ShapeDtypeStruct
WHOLE = pl.BlockSpec(memory_space=pltpu.VMEM)


def params(limit=16):
    return pltpu.CompilerParams(vmem_limit_bytes=limit << 20)


def cost(flops=0, nbytes=0):
    return pl.CostEstimate(flops=flops, bytes_accessed=nbytes, transcendentals=0)


def finish(matrix, panel, passed, place, block, inverse, gather, parts, arrived):
    height, width = matrix.shape
    swaps = arrived[0].shape[0]
    return pl.pallas_call(
        functools.partial(finish_kernel, len(parts), swaps),
        out_shape=SHAPE(matrix.shape, BF16),
        in_specs=[pl.BlockSpec(memory_space=pl.ANY)] + [WHOLE] * (6 + len(parts) + len(arrived)),
        out_specs=pl.BlockSpec(memory_space=pl.ANY),
        scratch_shapes=[
            pltpu.VMEM((height, width), BF16),
            pltpu.VMEM((height, NB + swaps), BF16),
            pltpu.VMEM((height, HALF), BF16),
            pltpu.VMEM((NB + swaps, width), BF16),
            pltpu.SemaphoreType.DMA((height // NB,)),
            pltpu.SemaphoreType.DMA((width // NB,)),
        ],
        compiler_params=params(20),
        name="finish",
    )(matrix, panel, passed, place, block, inverse, gather, *parts, *arrived)


def spread(value, axes, index, count):
    step = count // 2
    while step:
        pairs = [(i, i + step) for i in range(0, count, 2 * step)]
        received = lax.ppermute(value, axes, pairs)
        value = jnp.where(lax.rem(index, 2 * step) == step, received, value)
        step //= 2
    return value


def two_rounds(row_groups):
    outer, inner = grid_of(row_groups)

    def hops(pair):
        a, b = pair
        return abs(a // inner - b // inner) + abs(a % inner - b % inner)

    count = 0
    while (count + 1) ** 2 < row_groups:
        count += 1
    holders = [0, outer // 2 * inner]
    holders += [i for i in range(row_groups) if i not in holders][: count - 1]
    left = [i for i in range(row_groups) if i not in holders]
    second = []
    while left:
        pairs, free = [], list(holders)
        while free and left:
            best = min(((a, b) for a in free for b in left), key=hops)
            pairs.append(best)
            free.remove(best[0])
            left.remove(best[1])
        second.append(pairs)
    return [[(0, i)] for i in holders[1:]], second


def local(matrix, pivots):
    height, width = matrix.shape
    row_groups, col_groups = lax.axis_size("prow"), lax.axis_size("pcol")
    row_me, col_me = lax.axis_index("prow"), lax.axis_index("pcol")
    outer, inner = grid_of(row_groups)
    cap = round_rows(row_groups)
    smem = pl.BlockSpec(memory_space=pltpu.SMEM)

    rows_out = [SHAPE((1, NB), I32), SHAPE((1, NB), I32)]
    swap_scratch = [
        pltpu.SMEM((height * row_groups,), I32),
        pltpu.SMEM((1, NB), I32),
        pltpu.SMEM((1, NB), I32),
        pltpu.SemaphoreType.DMA,
        pltpu.SemaphoreType.DMA,
    ]
    rows, source, landing, *gives = pl.pallas_call(
        functools.partial(pick_kernel, row_groups, cap),
        out_shape=[SHAPE((cap, width), BF16)] + rows_out + [SHAPE((outer * cap, width), BF16)] * inner,
        in_specs=[smem, pl.BlockSpec(memory_space=pl.ANY)],
        out_specs=[WHOLE] * (3 + inner),
        scratch_shapes=[pltpu.VMEM((height, width), BF16)]
        + swap_scratch
        + [pltpu.SemaphoreType.DMA((height // NB,))],
        compiler_params=params(16),
        cost_estimate=cost(2 * 4 * cap * width * height, 20 << 20),
        name="pick",
    )(pivots, matrix)
    gather, place, flag = pl.pallas_call(
        functools.partial(tables_kernel, row_groups, cap),
        out_shape=[SHAPE((NB, row_groups * cap), BF16), SHAPE((1, HALF), I32), SHAPE((1, HALF), I32)],
        in_specs=[WHOLE] * 2,
        out_specs=[WHOLE] * 3,
        compiler_params=params(),
        cost_estimate=cost(1 << 35, 32 << 20),
        name="tables",
    )(source, landing)

    both = ("prow", "pcol")
    me = row_me * col_groups + col_me
    first_round, second_round = two_rounds(row_groups)

    def send(value, rounds):
        for pairs in rounds:
            yield pairs, lax.ppermute(value, both, [(a * col_groups, b * col_groups) for a, b in pairs])

    def take(value, received):
        for pairs, other in received:
            takes = functools.reduce(jnp.logical_or, [me == b * col_groups for _, b in pairs])
            value = jnp.where(takes, other, value)
        return value

    def at(o, i):
        return o % outer * inner + i % inner

    everyone = [(o, i) for o in range(outer) for i in range(inner)]

    block = matrix[:NB, :NB]
    received = list(send(block, first_round))

    parts = [rows]
    for step in range(1, outer):
        parts.append(lax.ppermute(rows, "prow", [(at(o, i), at(o + step, i)) for o, i in everyone]))
    bundles = [lax.ppermute(gives[j], "prow", [(0, j)]) for j in range(1, inner)]
    arrays, _ = lax.optimization_barrier(([other for _, other in received], place))
    block = take(block, [(pairs, other) for (pairs, _), other in zip(received, arrays)])
    block = take(block, list(send(block, second_round)))
    panel = jnp.concatenate([matrix[:, :NB], block], 0)
    half = col_groups // 2
    hop = lax.ppermute(panel, "pcol", [(0, half)])
    gathered, *sent = pl.pallas_call(
        functools.partial(turn_kernel, row_groups, cap),
        out_shape=[SHAPE((outer * cap, width), BF16)] + [SHAPE((cap, width), BF16)] * outer,
        in_specs=[WHOLE] * (outer + inner),
        out_specs=[WHOLE] * (1 + outer),
        compiler_params=params(8),
        name="turn",
    )(*parts, gives[0], *bundles)

    hop, sent = lax.optimization_barrier((hop, sent))
    panel = jnp.where(col_me == half, hop, panel)
    step = half // 2
    while step > 1:
        received = lax.ppermute(panel, "pcol", [(i, i + step) for i in range(0, col_groups, 2 * step)])
        panel = jnp.where(lax.rem(col_me, 2 * step) == step, received, panel)
        step //= 2

    parts = [gathered]
    for turn in range(1, inner):
        parts.append(lax.ppermute(gathered, "prow", [(at(o, i), at(o, i + turn)) for o, i in everyone]))
    arrived = [sent[0]]
    for step in range(1, outer):
        arrived.append(lax.ppermute(sent[step], "prow", [(i, at(step, i)) for i in range(inner)]))
    passed = lax.ppermute(panel, "pcol", [(i, i + 1) for i in range(0, col_groups, 2)])
    block = jnp.where(lax.rem(col_me, 2) == 1, passed[height:], panel[height:])
    inverse = pl.pallas_call(
        invert_kernel,
        out_shape=SHAPE((NB, HALF), F32),
        in_specs=[WHOLE],
        out_specs=WHOLE,
        cost_estimate=cost(2 * 60 * NB * NB * NB),
        name="invert",
    )(block)
    result = finish(matrix, panel, passed, place, block, inverse, gather, parts, arrived)

    def again(state):
        picked, place_all = pl.pallas_call(
            functools.partial(pick_all_kernel, row_groups),
            out_shape=[SHAPE((NB, width), BF16), SHAPE((1, NB), I32)],
            in_specs=[smem, WHOLE],
            out_specs=[WHOLE] * 2,
            scratch_shapes=[pltpu.VMEM((1, NB), I32)] * 2 + swap_scratch,
            compiler_params=params(),
            name="pick_all",
        )(pivots, matrix)
        top = picked
        for shift in range(1, row_groups):
            top = top + lax.ppermute(picked, "prow", [(i, (i + shift) % row_groups) for i in range(row_groups)])
        same = (iota((NB, NB), 0) == iota((NB, NB), 1)).astype(BF16)
        old_top = spread(matrix[:NB], "prow", row_me, row_groups)
        again_made = finish(matrix, panel, passed, place_all, block, inverse, same, [top], [old_top])
        return jnp.zeros((), jnp.bool_), again_made

    return lax.while_loop(lambda state: state[0], again, (flag[0, 0] > cap, result))[1]


def solution(mesh):
    placed = (P("prow", "pcol"), P())
    return jax.shard_map(
        local, mesh=mesh, in_specs=placed, out_specs=P("prow", "pcol"), check_vma=False
    )
```

time: 69.5 us -> 66.2 us (0.953)
  the two profiles are of different devices: /device:TPU:0 before, /device:TPU:6 now
where the time goes in v3:
time: 66.2 us; the launch traced here: 65.6 us
  starting transfers between devices  18.8 us (28%)
  Pallas kernels  18.7 us (28%)
  waiting for transfers between devices  18.7 us (28%)
  other arithmetic  5.86 us (9%)
  local copies, waits for them, and re-layouts  2.83 us (4%)
    ppermute x3, waiting for transfers between devices, local(): lax.ppermute(rows, 'prow', [(at(o, i), at(o + step, i)) for o, i in every...  13.9 us
    pallas_call x1, Pallas kernels, finish(): pl.pallas_call(functools.partial(finish_kernel, len(parts), swaps), out_s...  9.58 us
    ppermute x3, starting transfers between devices, local(): lax.ppermute(sent[step], 'prow', [(i, at(step, i)) for i in range(inner)])  6.82 us
    pallas_call x1, Pallas kernels, local(): pl.pallas_call(functools.partial(pick_kernel, row_groups, cap), out_shape...  5.75 us
    ppermute x1, waiting for transfers between devices, local(): lax.ppermute(gathered, 'prow', [(at(o, i), at(o, i + turn)) for o, i in e...  4.71 us
    ppermute x3, starting transfers between devices, local(): lax.ppermute(rows, 'prow', [(at(o, i), at(o + step, i)) for o, i in every...  4.08 us
    select_n x1, other arithmetic, local(): panel = jnp.where(col_me == half, hop, panel)  2.75 us
    pallas_call x1, Pallas kernels, local(): pl.pallas_call(invert_kernel, out_shape=SHAPE((NB, HALF), F32), in_specs=...  2.69 us
  transfers between devices with their start and end apart: 14, of which 4 were waited for; matrix products, arithmetic and copies ran while one was open for 3% of the time, Pallas kernels for 14%

profile of v3, /device:TPU:6, one launch (start us, length us, event | category | flops | bytes accessed | tf_op | source)
XLA Modules:
  0.0 65.6 jit_solution(9971107286641690296)
XLA Ops:
  0.0 0.9 %slice.20 = bf16[256,256]{1,0:T(8,128)(2,1)S(1)} slice(bf16[1792,1792]{1,0:T(8,128)(2,1)} %refs_0_.1), slice={[0:256], [0:256]} | slice | bytes 262144 | tf_op jit(solution)/shard_map/slice | solution.py:407
  0.9 0.7 %collective-permute-start.11 = (bf16[256,256]{1,0:T(8,128)(2,1)S(1)}, bf16[256,256]{1,0:T(8,128)(2,1)S(1)}, u32[]{:S(2)}, u32[]{:S(2)}) collective-permute-start(bf16[256,256]{1,0:T(8,128)(2,1)S(1)} %slice.20), channel_id=1, source_target_pairs={{0,4}} | collective-permute-start | bytes 393224 | tf_op jit(solution)/shard_map/ppermute | solution.py:394
  1.6 0.7 %collective-permute-start.10 = (bf16[256,256]{1,0:T(8,128)(2,1)S(1)}, bf16[256,256]{1,0:T(8,128)(2,1)S(1)}, u32[]{:S(2)}, u32[]{:S(2)}) collective-permute-start(bf16[256,256]{1,0:T(8,128)(2,1)S(1)} %slice.20), channel_id=1, source_target_pairs={{0,16}} | collective-permute-start | bytes 393224 | tf_op jit(solution)/shard_map/ppermute | solution.py:394
  2.3 5.8 %pick.1 = (bf16[48,1792]{1,0:T(8,128)(2,1)S(1)}, s32[1,256]{1,0:T(1,128)S(1)}, s32[1,256]{1,0:T(1,128)S(1)}, bf16[192,1792]{1,0:T(8,128)(2,1)S(1)}, bf16[192,1792]{1,0:T(8,128)(2,1)S(1)}) custom-call(s32[256]{0:T(256)} %pivots.1, bf16[1792,1792]{1,0:T(8,128)(2,1)} %refs_0_.1), custom_call_target="tpu_custom_call" | custom-call | flops 1233125376 | bytes 20971520 | tf_op jit(solution)/shard_map/pick/pallas_call | solution.py:366
  8.0 0.6 tables.1
  8.6 0.0 collective-permute-done.11
  8.6 0.0 collective-permute-done.10
  8.7 0.9 %select_select_fusion.1 = bf16[256,256]{1,0:T(8,128)(2,1)S(1)} fusion(bf16[256,256]{1,0:T(8,128)(2,1)S(1)} %collective-permute-done.11, bf16[256,256]{1,0:T(8,128)(2,1)S(1)} %collective-permute-done.10, pred[]{:T(512)S(6)} %eq.43, pred[]{:T(512)S(6)} %eq.42, bf16[1792,1792]{1,0:T(8,128)(2,1)} %refs_0_.1), kind=kLoop, calls=%fused_computation.10 | loop fusion | flops 131072 | bytes 524290 | tf_op jit(solution)/shard_map/jit(_where)/select_n | solution.py:399
  9.6 0.7 %collective-permute-start.13 = (bf16[256,256]{1,0:T(8,128)(2,1)S(1)}, bf16[256,256]{1,0:T(8,128)(2,1)S(1)}, u32[]{:S(2)}, u32[]{:S(2)}) collective-permute-start(bf16[256,256]{1,0:T(8,128)(2,1)S(1)} %select_select_fusion.1), channel_id=1, source_target_pairs={{0,8},{16,20},{4,12}} | collective-permute-start | bytes 393224 | tf_op jit(solution)/shard_map/ppermute | solution.py:394
  10.3 0.7 %collective-permute-start.12 = (bf16[256,256]{1,0:T(8,128)(2,1)S(1)}, bf16[256,256]{1,0:T(8,128)(2,1)S(1)}, u32[]{:S(2)}, u32[]{:S(2)}) collective-permute-start(bf16[256,256]{1,0:T(8,128)(2,1)S(1)} %select_select_fusion.1), channel_id=1, source_target_pairs={{16,24},{4,28}} | collective-permute-start | bytes 393224 | tf_op jit(solution)/shard_map/ppermute | solution.py:394
  10.9 1.2 %slice.19 = bf16[1792,256]{1,0:T(8,128)(2,1)S(1)} slice(bf16[1792,1792]{1,0:T(8,128)(2,1)} %refs_0_.1), slice={[0:1792], [0:256]} | slice | bytes 1835008 | tf_op jit(solution)/shard_map/slice | solution.py:417
  12.2 0.0 copy-start.2
  12.2 0.0 collective-permute-done.13
  12.2 0.0 collective-permute-done.12
  12.3 0.0 copy-start.3
  12.3 1.2 %pad_maximum_fusion = bf16[2048,256]{1,0:T(8,128)(2,1)} fusion(bf16[256,256]{1,0:T(8,128)(2,1)S(1)} %select_select_fusion, bf16[1792,256]{1,0:T(8,128)(2,1)S(1)} %slice.19), kind=kLoop, calls=%fused_computation.6 | loop fusion | flops 2097152 | bytes 2097152 | tf_op jit(solution)/shard_map/concatenate | solution.py:417
  13.5 1.3 %collective-permute-start.14 = (bf16[2048,256]{1,0:T(8,128)(2,1)}, bf16[2048,256]{1,0:T(8,128)(2,1)}, u32[]{:S(2)}, u32[]{:S(2)}) collective-permute-start(bf16[2048,256]{1,0:T(8,128)(2,1)} %pad_maximum_fusion), channel_id=1, source_target_pairs={{0,2},{4,6},{8,10},{12,14},{16,18},{20,22},{24,26},{28,30}} | collective-permute-start | bytes 3145736 | tf_op jit(solution)/shard_map/ppermute | solution.py:419
  14.7 0.0 copy-done.2
  14.8 1.3 %collective-permute-start.18 = (bf16[192,1792]{1,0:T(8,128)(2,1)S(1)}, bf16[192,1792]{1,0:T(8,128)(2,1)S(1)}, u32[]{:S(2)}, u32[]{:S(2)}) collective-permute-start(bf16[192,1792]{1,0:T(8,128)(2,1)S(1)} %get-tuple-element.80), channel_id=1, source_target_pairs={{0,4},{1,5},{2,6},{3,7}} | collective-permute-start | bytes 2064392 | tf_op jit(solution)/shard_map/ppermute | solution.py:413
  16.1 3.1 %collective-permute-start.17 = (bf16[48,1792]{1,0:T(8,128)(2,1)S(1)}, bf16[48,1792]{1,0:T(8,128)(2,1)S(1)}, u32[]{:S(2)}, u32[]{:S(2)}) collective-permute-start(bf16[48,1792]{1,0:T(8,128)(2,1)S(1)} %get-tuple-element.78.refs_0_), channel_id=1, source_target_pairs={{0,24},{4,28},{8,0},{12,4},{16,8},{20,12},{24,16},{28,20},{1,25},{... | collective-permute-start | bytes 516104 | tf_op jit(solution)/shard_map/ppermute | solution.py:412
  19.1 0.0 copy-done.3
  19.1 0.0 collective-permute-start.16
  19.1 1.0 %collective-permute-start.15 = (bf16[48,1792]{1,0:T(8,128)(2,1)S(1)}, bf16[48,1792]{1,0:T(8,128)(2,1)S(1)}, u32[]{:S(2)}, u32[]{:S(2)}) collective-permute-start(bf16[48,1792]{1,0:T(8,128)(2,1)S(1)} %get-tuple-element.78.refs_0_), channel_id=1, source_target_pairs={{0,8},{4,12},{8,16},{12,20},{16,24},{20,28},{24,0},{28,4},{1,9},{5... | collective-permute-start | bytes 516104 | tf_op jit(solution)/shard_map/ppermute | solution.py:412
  20.1 3.8 %collective-permute-done.17.refs_3_ = bf16[48,1792]{1,0:T(8,128)(2,1)S(1)} collective-permute-done((bf16[48,1792]{1,0:T(8,128)(2,1)S(1)}, bf16[48,1792]{1,0:T(8,128)(2,1)S(1)}, u32[]{:S(2)}, u32[]{:S(2)}) %collective-permute-start.17) | collective-permute-done | bytes 172064 | tf_op jit(solution)/shard_map/ppermute | solution.py:412
  24.0 10.1 %collective-permute-done.16.refs_2_ = bf16[48,1792]{1,0:T(8,128)(2,1)S(1)} collective-permute-done((bf16[48,1792]{1,0:T(8,128)(2,1)S(1)}, bf16[48,1792]{1,0:T(8,128)(2,1)S(1)}, u32[]{:S(2)}, u32[]{:S(2)}) %collective-permute-start.16) | collective-permute-done | bytes 172064 | tf_op jit(solution)/shard_map/ppermute | solution.py:412
  34.0 0.0 collective-permute-done.15.refs_1_
  34.0 0.1 collective-permute-done.18.refs_5_
  34.1 0.1 turn.1
  34.2 0.0 copy-start
  34.3 0.7 %copy-done = bf16[48,1792]{1,0:T(8,128)(2,1)} copy-done((bf16[48,1792]{1,0:T(8,128)(2,1)}, bf16[48,1792]{1,0:T(8,128)(2,1)S(1)}, u32[]{:S(2)}) %copy-start) | copy-done | bytes 172056
  34.9 0.0 collective-permute-done.14
  34.9 2.7 %broadcast_select_fusion.3.refs_1_ = bf16[2048,256]{1,0:T(8,128)(2,1)} fusion(bf16[2048,256]{1,0:T(8,128)(2,1)} %collective-permute-done.14, pred[]{:T(512)S(6)} %eq.39, bf16[256,256]{1,0:T(8,128)(2,1)} %copy-done.3, bf16[1792,256]{1,0:T(8,128)(2,1)} %copy-done.2), kind=kLoop, calls=%fused_computation.7 | loop fusion | flops 2621440 | bytes 3145729 | tf_op jit(solution)/shard_map/jit(_where)/select_n | solution.py:430
  37.7 2.3 %collective-permute-start.19 = (bf16[2048,256]{1,0:T(8,128)(2,1)}, bf16[2048,256]{1,0:T(8,128)(2,1)}, u32[]{:S(2)}, u32[]{:S(2)}) collective-permute-start(bf16[2048,256]{1,0:T(8,128)(2,1)} %broadcast_select_fusion.3.refs_1_), channel_id=1, source_target_pairs={{0,1},{2,3},{4,5},{6,7},{8,9},{10,11},{12,13},{14,15},{16,17},{18,... | collective-permute-start | bytes 3145736 | tf_op jit(solution)/shard_map/ppermute | solution.py:443
  39.9 0.4 collective-permute-start.20
  40.4 2.9 %collective-permute-start.21 = (bf16[48,1792]{1,0:T(8,128)(2,1)}, bf16[48,1792]{1,0:T(8,128)(2,1)S(1)}, u32[]{:S(2)}, u32[]{:S(2)}) collective-permute-start(bf16[48,1792]{1,0:T(8,128)(2,1)} %copy-done), channel_id=1, source_target_pairs={{0,8},{4,12},{1,9},{5,13},{2,10},{6,14},{3,11},{7,15}} | collective-permute-start | bytes 516104 | tf_op jit(solution)/shard_map/ppermute | solution.py:442
  43.3 2.6 %collective-permute-start.22 = (bf16[48,1792]{1,0:T(8,128)(2,1)S(1)}, bf16[48,1792]{1,0:T(8,128)(2,1)S(1)}, u32[]{:S(2)}, u32[]{:S(2)}) collective-permute-start(bf16[48,1792]{1,0:T(8,128)(2,1)S(1)} %get-tuple-element.90), channel_id=1, source_target_pairs={{0,16},{4,20},{1,17},{5,21},{2,18},{6,22},{3,19},{7,23}} | collective-permute-start | bytes 516104 | tf_op jit(solution)/shard_map/ppermute | solution.py:442
  45.9 1.3 %collective-permute-start.23 = (bf16[48,1792]{1,0:T(8,128)(2,1)S(1)}, bf16[48,1792]{1,0:T(8,128)(2,1)S(1)}, u32[]{:S(2)}, u32[]{:S(2)}) collective-permute-start(bf16[48,1792]{1,0:T(8,128)(2,1)S(1)} %get-tuple-element.91), channel_id=1, source_target_pairs={{0,24},{4,28},{1,25},{5,29},{2,26},{6,30},{3,27},{7,31}} | collective-permute-start | bytes 516104 | tf_op jit(solution)/shard_map/ppermute | solution.py:442
  47.3 0.0 collective-permute-done.19.refs_2_
  47.3 1.0 %slice_select_fusion.block.refs_4_ = bf16[256,256]{1,0:T(8,128)(2,1)S(1)} fusion(bf16[2048,256]{1,0:T(8,128)(2,1)} %broadcast_select_fusion.3.refs_1_, bf16[2048,256]{1,0:T(8,128)(2,1)} %collective-permute-done.19.refs_2_, pred[]{:T(512)S(6)} %eq.47), kind=kLoop, calls=%fused_computation.8 | loop fusion | flops 65536 | bytes 393217 | tf_op jit(solution)/shard_map/jit(_where)/select_n | solution.py:444
  48.3 2.7 %invert.1.refs_5_ = f32[256,128]{1,0:T(8,128)S(1)} custom-call(bf16[256,256]{1,0:T(8,128)(2,1)S(1)} %slice_select_fusion.block.refs_4_), custom_call_target="tpu_custom_call" | custom-call | flops 2013265920 | tf_op jit(solution)/shard_map/invert/pallas_call | solution.py:445
  50.9 4.7 %collective-permute-done.20.refs_8_ = bf16[192,1792]{1,0:T(8,128)(2,1)S(1)} collective-permute-done((bf16[192,1792]{1,0:T(8,128)(2,1)S(1)}, bf16[192,1792]{1,0:T(8,128)(2,1)S(1)}, u32[]{:S(2)}, u32[]{:S(2)}) %collective-permute-start.20) | collective-permute-done | bytes 688160 | tf_op jit(solution)/shard_map/ppermute | solution.py:439
  55.7 0.0 collective-permute-done.21.refs_10_
  55.7 0.0 collective-permute-done.22.refs_11_
  55.7 0.0 collective-permute-done.23.refs_12_
  55.7 0.0 copy-start.4
  55.7 9.6 %finish.3 = bf16[1792,1792]{1,0:T(8,128)(2,1)} custom-call(bf16[1792,1792]{1,0:T(8,128)(2,1)} %refs_0_.1, bf16[2048,256]{1,0:T(8,128)(2,1)} %broadcast_select_fusion.3.refs_1_, bf16[2048,256]{1,0:T(8,128)(2,1)} %collective-permute-done.19.refs_2_, s32[1,128]{1,0:T(1,128)S(1)} %get-tuple-element.75.refs_3_, ...), custom_call_target="tpu_custom_call" | custom-call | tf_op jit(solution)/shard_map/finish/pallas_call | solution.py:297
  65.3 0.0 copy-done.4
  65.3 0.2 while.9
  (1 shorter events, 0.0 us)
Async XLA Ops:
  0.9 7.7 %collective-permute-start.11 = (bf16[256,256]{1,0:T(8,128)(2,1)S(1)}, bf16[256,256]{1,0:T(8,128)(2,1)S(1)}, u32[]{:S(2)}, u32[]{:S(2)}) collective-permute-start(bf16[256,256]{1,0:T(8,128)(2,1)S(1)} %slice.20), channel_id=1, source_target_pairs={{0,4}} | collective-permute-start | bytes 393224 | tf_op jit(solution)/shard_map/ppermute | solution.py:394
  1.6 7.1 %collective-permute-start.10 = (bf16[256,256]{1,0:T(8,128)(2,1)S(1)}, bf16[256,256]{1,0:T(8,128)(2,1)S(1)}, u32[]{:S(2)}, u32[]{:S(2)}) collective-permute-start(bf16[256,256]{1,0:T(8,128)(2,1)S(1)} %slice.20), channel_id=1, source_target_pairs={{0,16}} | collective-permute-start | bytes 393224 | tf_op jit(solution)/shard_map/ppermute | solution.py:394
  9.6 2.6 %collective-permute-start.13 = (bf16[256,256]{1,0:T(8,128)(2,1)S(1)}, bf16[256,256]{1,0:T(8,128)(2,1)S(1)}, u32[]{:S(2)}, u32[]{:S(2)}) collective-permute-start(bf16[256,256]{1,0:T(8,128)(2,1)S(1)} %select_select_fusion.1), channel_id=1, source_target_pairs={{0,8},{16,20},{4,12}} | collective-permute-start | bytes 393224 | tf_op jit(solution)/shard_map/ppermute | solution.py:394
  10.3 2.0 %collective-permute-start.12 = (bf16[256,256]{1,0:T(8,128)(2,1)S(1)}, bf16[256,256]{1,0:T(8,128)(2,1)S(1)}, u32[]{:S(2)}, u32[]{:S(2)}) collective-permute-start(bf16[256,256]{1,0:T(8,128)(2,1)S(1)} %select_select_fusion.1), channel_id=1, source_target_pairs={{16,24},{4,28}} | collective-permute-start | bytes 393224 | tf_op jit(solution)/shard_map/ppermute | solution.py:394
  12.2 2.6 %copy-start.2 = (bf16[1792,256]{1,0:T(8,128)(2,1)}, bf16[1792,256]{1,0:T(8,128)(2,1)S(1)}, u32[]{:S(2)}) copy-start(bf16[1792,256]{1,0:T(8,128)(2,1)S(1)} %slice.19) | copy-start | bytes 2752516
  12.3 6.9 %copy-start.3 = (bf16[256,256]{1,0:T(8,128)(2,1)}, bf16[256,256]{1,0:T(8,128)(2,1)S(1)}, u32[]{:S(2)}) copy-start(bf16[256,256]{1,0:T(8,128)(2,1)S(1)} %select_select_fusion) | copy-start | bytes 393220
  13.5 21.5 %collective-permute-start.14 = (bf16[2048,256]{1,0:T(8,128)(2,1)}, bf16[2048,256]{1,0:T(8,128)(2,1)}, u32[]{:S(2)}, u32[]{:S(2)}) collective-permute-start(bf16[2048,256]{1,0:T(8,128)(2,1)} %pad_maximum_fusion), channel_id=1, source_target_pairs={{0,2},{4,6},{8,10},{12,14},{16,18},{20,22},{24,26},{28,30}} | collective-permute-start | bytes 3145736 | tf_op jit(solution)/shard_map/ppermute | solution.py:419
  14.8 19.4 %collective-permute-start.18 = (bf16[192,1792]{1,0:T(8,128)(2,1)S(1)}, bf16[192,1792]{1,0:T(8,128)(2,1)S(1)}, u32[]{:S(2)}, u32[]{:S(2)}) collective-permute-start(bf16[192,1792]{1,0:T(8,128)(2,1)S(1)} %get-tuple-element.80), channel_id=1, source_target_pairs={{0,4},{1,5},{2,6},{3,7}} | collective-permute-start | bytes 2064392 | tf_op jit(solution)/shard_map/ppermute | solution.py:413
  16.1 7.9 %collective-permute-start.17 = (bf16[48,1792]{1,0:T(8,128)(2,1)S(1)}, bf16[48,1792]{1,0:T(8,128)(2,1)S(1)}, u32[]{:S(2)}, u32[]{:S(2)}) collective-permute-start(bf16[48,1792]{1,0:T(8,128)(2,1)S(1)} %get-tuple-element.78.refs_0_), channel_id=1, source_target_pairs={{0,24},{4,28},{8,0},{12,4},{16,8},{20,12},{24,16},{28,20},{1,25},{... | collective-permute-start | bytes 516104 | tf_op jit(solution)/shard_map/ppermute | solution.py:412
  19.1 14.9 %collective-permute-start.16 = (bf16[48,1792]{1,0:T(8,128)(2,1)S(1)}, bf16[48,1792]{1,0:T(8,128)(2,1)S(1)}, u32[]{:S(2)}, u32[]{:S(2)}) collective-permute-start(bf16[48,1792]{1,0:T(8,128)(2,1)S(1)} %get-tuple-element.78.refs_0_), channel_id=1, source_target_pairs={{0,16},{4,20},{8,24},{12,28},{16,0},{20,4},{24,8},{28,12},{1,17},{... | collective-permute-start | bytes 516104 | tf_op jit(solution)/shard_map/ppermute | solution.py:412
  19.1 14.9 %collective-permute-start.15 = (bf16[48,1792]{1,0:T(8,128)(2,1)S(1)}, bf16[48,1792]{1,0:T(8,128)(2,1)S(1)}, u32[]{:S(2)}, u32[]{:S(2)}) collective-permute-start(bf16[48,1792]{1,0:T(8,128)(2,1)S(1)} %get-tuple-element.78.refs_0_), channel_id=1, source_target_pairs={{0,8},{4,12},{8,16},{12,20},{16,24},{20,28},{24,0},{28,4},{1,9},{5... | collective-permute-start | bytes 516104 | tf_op jit(solution)/shard_map/ppermute | solution.py:412
  34.2 0.7 %copy-start = (bf16[48,1792]{1,0:T(8,128)(2,1)}, bf16[48,1792]{1,0:T(8,128)(2,1)S(1)}, u32[]{:S(2)}) copy-start(bf16[48,1792]{1,0:T(8,128)(2,1)S(1)} %get-tuple-element.89) | copy-start | bytes 516100
  37.7 9.6 %collective-permute-start.19 = (bf16[2048,256]{1,0:T(8,128)(2,1)}, bf16[2048,256]{1,0:T(8,128)(2,1)}, u32[]{:S(2)}, u32[]{:S(2)}) collective-permute-start(bf16[2048,256]{1,0:T(8,128)(2,1)} %broadcast_select_fusion.3.refs_1_), channel_id=1, source_target_pairs={{0,1},{2,3},{4,5},{6,7},{8,9},{10,11},{12,13},{14,15},{16,17},{18,... | collective-permute-start | bytes 3145736 | tf_op jit(solution)/shard_map/ppermute | solution.py:443
  39.9 15.7 %collective-permute-start.20 = (bf16[192,1792]{1,0:T(8,128)(2,1)S(1)}, bf16[192,1792]{1,0:T(8,128)(2,1)S(1)}, u32[]{:S(2)}, u32[]{:S(2)}) collective-permute-start(bf16[192,1792]{1,0:T(8,128)(2,1)S(1)} %get-tuple-element.87.refs_7_), channel_id=1, source_target_pairs={{0,4},{4,0},{8,12},{12,8},{16,20},{20,16},{24,28},{28,24},{1,5},{5... | collective-permute-start | bytes 2064392 | tf_op jit(solution)/shard_map/ppermute | solution.py:439
  40.4 15.3 %collective-permute-start.21 = (bf16[48,1792]{1,0:T(8,128)(2,1)}, bf16[48,1792]{1,0:T(8,128)(2,1)S(1)}, u32[]{:S(2)}, u32[]{:S(2)}) collective-permute-start(bf16[48,1792]{1,0:T(8,128)(2,1)} %copy-done), channel_id=1, source_target_pairs={{0,8},{4,12},{1,9},{5,13},{2,10},{6,14},{3,11},{7,15}} | collective-permute-start | bytes 516104 | tf_op jit(solution)/shard_map/ppermute | solution.py:442
  43.3 12.3 %collective-permute-start.22 = (bf16[48,1792]{1,0:T(8,128)(2,1)S(1)}, bf16[48,1792]{1,0:T(8,128)(2,1)S(1)}, u32[]{:S(2)}, u32[]{:S(2)}) collective-permute-start(bf16[48,1792]{1,0:T(8,128)(2,1)S(1)} %get-tuple-element.90), channel_id=1, source_target_pairs={{0,16},{4,20},{1,17},{5,21},{2,18},{6,22},{3,19},{7,23}} | collective-permute-start | bytes 516104 | tf_op jit(solution)/shard_map/ppermute | solution.py:442
  45.9 9.7 %collective-permute-start.23 = (bf16[48,1792]{1,0:T(8,128)(2,1)S(1)}, bf16[48,1792]{1,0:T(8,128)(2,1)S(1)}, u32[]{:S(2)}, u32[]{:S(2)}) collective-permute-start(bf16[48,1792]{1,0:T(8,128)(2,1)S(1)} %get-tuple-element.91), channel_id=1, source_target_pairs={{0,24},{4,28},{1,25},{5,29},{2,26},{6,30},{3,27},{7,31}} | collective-permute-start | bytes 516104 | tf_op jit(solution)/shard_map/ppermute | solution.py:442
  55.7 9.6 %copy-start.4 = (s32[256]{0:T(256)S(1)}, s32[256]{0:T(256)}, u32[]{:S(2)}) copy-start(s32[256]{0:T(256)} %pivots.1) | copy-start | bytes 3076

commit v4 on v3

--- a/solution.py
+++ b/solution.py
@@ -426,7 +426,7 @@
         name="turn",
     )(*parts, gives[0], *bundles)
 
-    hop, sent = lax.optimization_barrier((hop, sent))
+    hop, _ = lax.optimization_barrier((hop, (parts[-1], bundles)))
     panel = jnp.where(col_me == half, hop, panel)
     step = half // 2
     while step > 1:

time: 66.2 us -> 76.9 us (1.16)
  waiting for transfers between devices: 18.7 us -> 28.9 us
  starting transfers between devices: 18.8 us -> 20.2 us
    ppermute x1, waiting for transfers between devices: 0.1 us -> 11.1 us  [local(): lax.ppermute(gives[j], 'prow', [(0, j)])]
    ppermute x3, waiting for transfers between devices: 13.9 us -> 9.93 us  [local(): lax.ppermute(rows, 'prow', [(at(o, i), at(o + step, i)) for o, i in every...]
    ppermute x3, starting transfers between devices: 4.08 us -> 7.89 us  [local(): lax.ppermute(rows, 'prow', [(at(o, i), at(o + step, i)) for o, i in every...]
    ppermute x3, waiting for transfers between devices: 0.01 us -> 3.21 us  [local(): lax.ppermute(sent[step], 'prow', [(i, at(step, i)) for i in range(inner)])]
    ppermute x3, starting transfers between devices: 6.82 us -> 4.78 us  [local(): lax.ppermute(sent[step], 'prow', [(i, at(step, i)) for i in range(inner)])]
  transfers between devices with their start and end apart: 14 -> 14, of which waited for: 4 -> 7; matrix products, arithmetic and copies ran while one was open for 3% -> 3% of each run, Pallas kernels for 14% -> 12%
where the time goes in v4:
time: 76.9 us; the launch traced here: 76.5 us
  waiting for transfers between devices  28.9 us (38%)
  starting transfers between devices  20.2 us (26%)
  Pallas kernels  18.7 us (24%)
  other arithmetic  5.83 us (8%)
  local copies, waits for them, and re-layouts  2.16 us (3%)
    ppermute x1, waiting for transfers between devices, local(): lax.ppermute(gives[j], 'prow', [(0, j)])  11.1 us
    ppermute x3, waiting for transfers between devices, local(): lax.ppermute(rows, 'prow', [(at(o, i), at(o + step, i)) for o, i in every...  9.93 us
    pallas_call x1, Pallas kernels, finish(): pl.pallas_call(functools.partial(finish_kernel, len(parts), swaps), out_s...  9.58 us
    ppermute x3, starting transfers between devices, local(): lax.ppermute(rows, 'prow', [(at(o, i), at(o + step, i)) for o, i in every...  7.89 us
    pallas_call x1, Pallas kernels, local(): pl.pallas_call(functools.partial(pick_kernel, row_groups, cap), out_shape...  5.75 us
    ppermute x3, starting transfers between devices, local(): lax.ppermute(sent[step], 'prow', [(i, at(step, i)) for i in range(inner)])  4.78 us
    ppermute x1, waiting for transfers between devices, local(): lax.ppermute(gathered, 'prow', [(at(o, i), at(o, i + turn)) for o, i in e...  4.55 us
    ppermute x3, waiting for transfers between devices, local(): lax.ppermute(sent[step], 'prow', [(i, at(step, i)) for i in range(inner)])  3.21 us
  transfers between devices with their start and end apart: 14, of which 7 were waited for; matrix products, arithmetic and copies ran while one was open for 3% of the time, Pallas kernels for 12%

profile of v4, /device:TPU:6, one launch (start us, length us, event | category | flops | bytes accessed | tf_op | source)
XLA Modules:
  0.0 76.5 jit_solution(15746309895565563211)
XLA Ops:
  0.0 0.9 %slice.20 = bf16[256,256]{1,0:T(8,128)(2,1)S(1)} slice(bf16[1792,1792]{1,0:T(8,128)(2,1)} %refs_0_.1), slice={[0:256], [0:256]} | slice | bytes 262144 | tf_op jit(solution)/shard_map/slice | solution.py:407
  0.9 0.7 collective-permute-start.11
  1.6 0.7 collective-permute-start.10
  2.3 5.8 %pick.1 = (bf16[48,1792]{1,0:T(8,128)(2,1)S(1)}, s32[1,256]{1,0:T(1,128)S(1)}, s32[1,256]{1,0:T(1,128)S(1)}, bf16[192,1792]{1,0:T(8,128)(2,1)S(1)}, bf16[192,1792]{1,0:T(8,128)(2,1)S(1)}) custom-call(s32[256]{0:T(256)} %pivots.1, bf16[1792,1792]{1,0:T(8,128)(2,1)} %refs_0_.1), custom_call_target="tpu_custom_call" | custom-call | flops 1233125376 | bytes 20971520 | tf_op jit(solution)/shard_map/pick/pallas_call | solution.py:366
  8.0 0.6 tables.1
  8.6 0.0 collective-permute-done.11
  8.6 0.0 collective-permute-done.10
  8.7 0.9 %select_select_fusion.1 = bf16[256,256]{1,0:T(8,128)(2,1)S(1)} fusion(bf16[256,256]{1,0:T(8,128)(2,1)S(1)} %collective-permute-done.11, bf16[256,256]{1,0:T(8,128)(2,1)S(1)} %collective-permute-done.10, pred[]{:T(512)S(6)} %eq.43, pred[]{:T(512)S(6)} %eq.42, bf16[1792,1792]{1,0:T(8,128)(2,1)} %refs_0_.1), kind=kLoop, calls=%fused_computation.10 | loop fusion | flops 131072 | bytes 524290 | tf_op jit(solution)/shard_map/jit(_where)/select_n | solution.py:399
  9.6 0.7 collective-permute-start.13
  10.3 0.7 collective-permute-start.12
  10.9 1.2 %slice.19 = bf16[1792,256]{1,0:T(8,128)(2,1)S(1)} slice(bf16[1792,1792]{1,0:T(8,128)(2,1)} %refs_0_.1), slice={[0:1792], [0:256]} | slice | bytes 1835008 | tf_op jit(solution)/shard_map/slice | solution.py:417
  12.2 0.0 copy-start.1
  12.2 0.0 collective-permute-done.13
  12.2 0.0 collective-permute-done.12
  12.3 1.2 %pad_maximum_fusion = bf16[2048,256]{1,0:T(8,128)(2,1)} fusion(bf16[256,256]{1,0:T(8,128)(2,1)S(1)} %select_select_fusion, bf16[1792,256]{1,0:T(8,128)(2,1)S(1)} %slice.19), kind=kLoop, calls=%fused_computation.6 | loop fusion | flops 2097152 | bytes 2097152 | tf_op jit(solution)/shard_map/concatenate | solution.py:417
  13.4 1.3 %collective-permute-start.14 = (bf16[2048,256]{1,0:T(8,128)(2,1)}, bf16[2048,256]{1,0:T(8,128)(2,1)}, u32[]{:S(2)}, u32[]{:S(2)}) collective-permute-start(bf16[2048,256]{1,0:T(8,128)(2,1)} %pad_maximum_fusion), channel_id=1, source_target_pairs={{0,2},{4,6},{8,10},{12,14},{16,18},{20,22},{24,26},{28,30}} | collective-permute-start | bytes 3145736 | tf_op jit(solution)/shard_map/ppermute | solution.py:419
  14.7 0.0 copy-done.1
  14.7 1.3 %collective-permute-start.16 = (bf16[192,1792]{1,0:T(8,128)(2,1)S(1)}, bf16[192,1792]{1,0:T(8,128)(2,1)S(1)}, u32[]{:S(2)}, u32[]{:S(2)}) collective-permute-start(bf16[192,1792]{1,0:T(8,128)(2,1)S(1)} %get-tuple-element.75), channel_id=1, source_target_pairs={{0,4},{1,5},{2,6},{3,7}} | collective-permute-start | bytes 2064392 | tf_op jit(solution)/shard_map/ppermute | solution.py:413
  16.0 3.1 %collective-permute-start.15 = (bf16[48,1792]{1,0:T(8,128)(2,1)S(1)}, bf16[48,1792]{1,0:T(8,128)(2,1)S(1)}, u32[]{:S(2)}, u32[]{:S(2)}) collective-permute-start(bf16[48,1792]{1,0:T(8,128)(2,1)S(1)} %get-tuple-element.74.refs_0_), channel_id=1, source_target_pairs={{0,24},{4,28},{8,0},{12,4},{16,8},{20,12},{24,16},{28,20},{1,25},{... | collective-permute-start | bytes 516104 | tf_op jit(solution)/shard_map/ppermute | solution.py:412
  19.1 3.9 %collective-permute-done.15.refs_3_ = bf16[48,1792]{1,0:T(8,128)(2,1)S(1)} collective-permute-done((bf16[48,1792]{1,0:T(8,128)(2,1)S(1)}, bf16[48,1792]{1,0:T(8,128)(2,1)S(1)}, u32[]{:S(2)}, u32[]{:S(2)}) %collective-permute-start.15) | collective-permute-done | bytes 172064 | tf_op jit(solution)/shard_map/ppermute | solution.py:412
  23.1 11.1 %collective-permute-done.16.refs_5_ = bf16[192,1792]{1,0:T(8,128)(2,1)S(1)} collective-permute-done((bf16[192,1792]{1,0:T(8,128)(2,1)S(1)}, bf16[192,1792]{1,0:T(8,128)(2,1)S(1)}, u32[]{:S(2)}, u32[]{:S(2)}) %collective-permute-start.16) | collective-permute-done | bytes 688160 | tf_op jit(solution)/shard_map/ppermute | solution.py:413
  34.1 0.1 collective-permute-done.14
  34.2 2.7 %broadcast_select_fusion.3.refs_1_ = bf16[2048,256]{1,0:T(8,128)(2,1)} fusion(bf16[2048,256]{1,0:T(8,128)(2,1)} %collective-permute-done.14, pred[]{:T(512)S(6)} %eq.39, bf16[256,256]{1,0:T(8,128)(2,1)S(1)} %select_select_fusion, bf16[1792,256]{1,0:T(8,128)(2,1)} %copy-done.1), kind=kLoop, calls=%fused_computation.7 | loop fusion | flops 2621440 | bytes 3145729 | tf_op jit(solution)/shard_map/jit(_where)/select_n | solution.py:430
  37.0 2.2 %collective-permute-start.17 = (bf16[2048,256]{1,0:T(8,128)(2,1)}, bf16[2048,256]{1,0:T(8,128)(2,1)}, u32[]{:S(2)}, u32[]{:S(2)}) collective-permute-start(bf16[2048,256]{1,0:T(8,128)(2,1)} %broadcast_select_fusion.3.refs_1_), channel_id=1, source_target_pairs={{0,1},{2,3},{4,5},{6,7},{8,9},{10,11},{12,13},{14,15},{16,17},{18,... | collective-permute-start | bytes 3145736 | tf_op jit(solution)/shard_map/ppermute | solution.py:443
  39.2 0.8 %collective-permute-start.19 = (bf16[48,1792]{1,0:T(8,128)(2,1)S(1)}, bf16[48,1792]{1,0:T(8,128)(2,1)S(1)}, u32[]{:S(2)}, u32[]{:S(2)}) collective-permute-start(bf16[48,1792]{1,0:T(8,128)(2,1)S(1)} %get-tuple-element.74.refs_0_), channel_id=1, source_target_pairs={{0,16},{4,20},{8,24},{12,28},{16,0},{20,4},{24,8},{28,12},{1,17},{... | collective-permute-start | bytes 516104 | tf_op jit(solution)/shard_map/ppermute | solution.py:412
  40.0 4.0 %collective-permute-start.18 = (bf16[48,1792]{1,0:T(8,128)(2,1)S(1)}, bf16[48,1792]{1,0:T(8,128)(2,1)S(1)}, u32[]{:S(2)}, u32[]{:S(2)}) collective-permute-start(bf16[48,1792]{1,0:T(8,128)(2,1)S(1)} %get-tuple-element.74.refs_0_), channel_id=1, source_target_pairs={{0,8},{4,12},{8,16},{12,20},{16,24},{20,28},{24,0},{28,4},{1,9},{5... | collective-permute-start | bytes 516104 | tf_op jit(solution)/shard_map/ppermute | solution.py:412
  44.0 6.0 %collective-permute-done.19.refs_2_ = bf16[48,1792]{1,0:T(8,128)(2,1)S(1)} collective-permute-done((bf16[48,1792]{1,0:T(8,128)(2,1)S(1)}, bf16[48,1792]{1,0:T(8,128)(2,1)S(1)}, u32[]{:S(2)}, u32[]{:S(2)}) %collective-permute-start.19) | collective-permute-done | bytes 172064 | tf_op jit(solution)/shard_map/ppermute | solution.py:412
  50.0 0.0 collective-permute-done.18.refs_1_
  50.0 0.1 turn.1
  50.1 0.1 collective-permute-start.20
  50.2 1.3 %collective-permute-start.21 = (bf16[48,1792]{1,0:T(8,128)(2,1)S(1)}, bf16[48,1792]{1,0:T(8,128)(2,1)S(1)}, u32[]{:S(2)}, u32[]{:S(2)}) collective-permute-start(bf16[48,1792]{1,0:T(8,128)(2,1)S(1)} %get-tuple-element.81), channel_id=1, source_target_pairs={{0,8},{4,12},{1,9},{5,13},{2,10},{6,14},{3,11},{7,15}} | collective-permute-start | bytes 516104 | tf_op jit(solution)/shard_map/ppermute | solution.py:442
  51.6 2.1 %collective-permute-start.22 = (bf16[48,1792]{1,0:T(8,128)(2,1)S(1)}, bf16[48,1792]{1,0:T(8,128)(2,1)S(1)}, u32[]{:S(2)}, u32[]{:S(2)}) collective-permute-start(bf16[48,1792]{1,0:T(8,128)(2,1)S(1)} %get-tuple-element.82), channel_id=1, source_target_pairs={{0,16},{4,20},{1,17},{5,21},{2,18},{6,22},{3,19},{7,23}} | collective-permute-start | bytes 516104 | tf_op jit(solution)/shard_map/ppermute | solution.py:442
  53.7 1.3 %collective-permute-start.23 = (bf16[48,1792]{1,0:T(8,128)(2,1)S(1)}, bf16[48,1792]{1,0:T(8,128)(2,1)S(1)}, u32[]{:S(2)}, u32[]{:S(2)}) collective-permute-start(bf16[48,1792]{1,0:T(8,128)(2,1)S(1)} %get-tuple-element.83), channel_id=1, source_target_pairs={{0,24},{4,28},{1,25},{5,29},{2,26},{6,30},{3,27},{7,31}} | collective-permute-start | bytes 516104 | tf_op jit(solution)/shard_map/ppermute | solution.py:442
  55.0 0.0 collective-permute-done.17.refs_2_
  55.0 1.0 %slice_select_fusion.block.refs_4_ = bf16[256,256]{1,0:T(8,128)(2,1)S(1)} fusion(bf16[2048,256]{1,0:T(8,128)(2,1)} %broadcast_select_fusion.3.refs_1_, bf16[2048,256]{1,0:T(8,128)(2,1)} %collective-permute-done.17.refs_2_, pred[]{:T(512)S(6)} %eq.47), kind=kLoop, calls=%fused_computation.8 | loop fusion | flops 65536 | bytes 393217 | tf_op jit(solution)/shard_map/jit(_where)/select_n | solution.py:444
  56.0 2.7 %invert.1.refs_5_ = f32[256,128]{1,0:T(8,128)S(1)} custom-call(bf16[256,256]{1,0:T(8,128)(2,1)S(1)} %slice_select_fusion.block.refs_4_), custom_call_target="tpu_custom_call" | custom-call | flops 2013265920 | tf_op jit(solution)/shard_map/invert/pallas_call | solution.py:445
  58.7 0.0 collective-permute-done.21.refs_10_
  58.7 1.3 %collective-permute-done.22.refs_11_ = bf16[48,1792]{1,0:T(8,128)(2,1)S(1)} collective-permute-done((bf16[48,1792]{1,0:T(8,128)(2,1)S(1)}, bf16[48,1792]{1,0:T(8,128)(2,1)S(1)}, u32[]{:S(2)}, u32[]{:S(2)}) %collective-permute-start.22) | collective-permute-done | bytes 172064 | tf_op jit(solution)/shard_map/ppermute | solution.py:442
  60.1 1.9 %collective-permute-done.23.refs_12_ = bf16[48,1792]{1,0:T(8,128)(2,1)S(1)} collective-permute-done((bf16[48,1792]{1,0:T(8,128)(2,1)S(1)}, bf16[48,1792]{1,0:T(8,128)(2,1)S(1)}, u32[]{:S(2)}, u32[]{:S(2)}) %collective-permute-start.23) | collective-permute-done | bytes 172064 | tf_op jit(solution)/shard_map/ppermute | solution.py:442
  62.0 4.6 %collective-permute-done.20.refs_8_ = bf16[192,1792]{1,0:T(8,128)(2,1)S(1)} collective-permute-done((bf16[192,1792]{1,0:T(8,128)(2,1)S(1)}, bf16[192,1792]{1,0:T(8,128)(2,1)S(1)}, u32[]{:S(2)}, u32[]{:S(2)}) %collective-permute-start.20) | collective-permute-done | bytes 688160 | tf_op jit(solution)/shard_map/ppermute | solution.py:439
  66.5 0.0 copy-start.2
  66.5 9.6 %finish.3 = bf16[1792,1792]{1,0:T(8,128)(2,1)} custom-call(bf16[1792,1792]{1,0:T(8,128)(2,1)} %refs_0_.1, bf16[2048,256]{1,0:T(8,128)(2,1)} %broadcast_select_fusion.3.refs_1_, bf16[2048,256]{1,0:T(8,128)(2,1)} %collective-permute-done.17.refs_2_, s32[1,128]{1,0:T(1,128)S(1)} %get-tuple-element.71.refs_3_, ...), custom_call_target="tpu_custom_call" | custom-call | tf_op jit(solution)/shard_map/finish/pallas_call | solution.py:297
  76.1 0.0 copy-done.2
  76.1 0.2 while.9
  (1 shorter events, 0.0 us)
Async XLA Ops:
  0.9 7.7 %collective-permute-start.11 = (bf16[256,256]{1,0:T(8,128)(2,1)S(1)}, bf16[256,256]{1,0:T(8,128)(2,1)S(1)}, u32[]{:S(2)}, u32[]{:S(2)}) collective-permute-start(bf16[256,256]{1,0:T(8,128)(2,1)S(1)} %slice.20), channel_id=1, source_target_pairs={{0,4}} | collective-permute-start | bytes 393224 | tf_op jit(solution)/shard_map/ppermute | solution.py:394
  1.6 7.1 %collective-permute-start.10 = (bf16[256,256]{1,0:T(8,128)(2,1)S(1)}, bf16[256,256]{1,0:T(8,128)(2,1)S(1)}, u32[]{:S(2)}, u32[]{:S(2)}) collective-permute-start(bf16[256,256]{1,0:T(8,128)(2,1)S(1)} %slice.20), channel_id=1, source_target_pairs={{0,16}} | collective-permute-start | bytes 393224 | tf_op jit(solution)/shard_map/ppermute | solution.py:394
  9.6 2.6 %collective-permute-start.13 = (bf16[256,256]{1,0:T(8,128)(2,1)S(1)}, bf16[256,256]{1,0:T(8,128)(2,1)S(1)}, u32[]{:S(2)}, u32[]{:S(2)}) collective-permute-start(bf16[256,256]{1,0:T(8,128)(2,1)S(1)} %select_select_fusion.1), channel_id=1, source_target_pairs={{0,8},{16,20},{4,12}} | collective-permute-start | bytes 393224 | tf_op jit(solution)/shard_map/ppermute | solution.py:394
  10.3 2.0 %collective-permute-start.12 = (bf16[256,256]{1,0:T(8,128)(2,1)S(1)}, bf16[256,256]{1,0:T(8,128)(2,1)S(1)}, u32[]{:S(2)}, u32[]{:S(2)}) collective-permute-start(bf16[256,256]{1,0:T(8,128)(2,1)S(1)} %select_select_fusion.1), channel_id=1, source_target_pairs={{16,24},{4,28}} | collective-permute-start | bytes 393224 | tf_op jit(solution)/shard_map/ppermute | solution.py:394
  12.2 2.5 %copy-start.1 = (bf16[1792,256]{1,0:T(8,128)(2,1)}, bf16[1792,256]{1,0:T(8,128)(2,1)S(1)}, u32[]{:S(2)}) copy-start(bf16[1792,256]{1,0:T(8,128)(2,1)S(1)} %slice.19) | copy-start | bytes 2752516
  13.4 20.8 %collective-permute-start.14 = (bf16[2048,256]{1,0:T(8,128)(2,1)}, bf16[2048,256]{1,0:T(8,128)(2,1)}, u32[]{:S(2)}, u32[]{:S(2)}) collective-permute-start(bf16[2048,256]{1,0:T(8,128)(2,1)} %pad_maximum_fusion), channel_id=1, source_target_pairs={{0,2},{4,6},{8,10},{12,14},{16,18},{20,22},{24,26},{28,30}} | collective-permute-start | bytes 3145736 | tf_op jit(solution)/shard_map/ppermute | solution.py:419
  14.7 19.4 %collective-permute-start.16 = (bf16[192,1792]{1,0:T(8,128)(2,1)S(1)}, bf16[192,1792]{1,0:T(8,128)(2,1)S(1)}, u32[]{:S(2)}, u32[]{:S(2)}) collective-permute-start(bf16[192,1792]{1,0:T(8,128)(2,1)S(1)} %get-tuple-element.75), channel_id=1, source_target_pairs={{0,4},{1,5},{2,6},{3,7}} | collective-permute-start | bytes 2064392 | tf_op jit(solution)/shard_map/ppermute | solution.py:413
  16.0 7.0 %collective-permute-start.15 = (bf16[48,1792]{1,0:T(8,128)(2,1)S(1)}, bf16[48,1792]{1,0:T(8,128)(2,1)S(1)}, u32[]{:S(2)}, u32[]{:S(2)}) collective-permute-start(bf16[48,1792]{1,0:T(8,128)(2,1)S(1)} %get-tuple-element.74.refs_0_), channel_id=1, source_target_pairs={{0,24},{4,28},{8,0},{12,4},{16,8},{20,12},{24,16},{28,20},{1,25},{... | collective-permute-start | bytes 516104 | tf_op jit(solution)/shard_map/ppermute | solution.py:412
  37.0 18.1 %collective-permute-start.17 = (bf16[2048,256]{1,0:T(8,128)(2,1)}, bf16[2048,256]{1,0:T(8,128)(2,1)}, u32[]{:S(2)}, u32[]{:S(2)}) collective-permute-start(bf16[2048,256]{1,0:T(8,128)(2,1)} %broadcast_select_fusion.3.refs_1_), channel_id=1, source_target_pairs={{0,1},{2,3},{4,5},{6,7},{8,9},{10,11},{12,13},{14,15},{16,17},{18,... | collective-permute-start | bytes 3145736 | tf_op jit(solution)/shard_map/ppermute | solution.py:443
  39.2 10.8 %collective-permute-start.19 = (bf16[48,1792]{1,0:T(8,128)(2,1)S(1)}, bf16[48,1792]{1,0:T(8,128)(2,1)S(1)}, u32[]{:S(2)}, u32[]{:S(2)}) collective-permute-start(bf16[48,1792]{1,0:T(8,128)(2,1)S(1)} %get-tuple-element.74.refs_0_), channel_id=1, source_target_pairs={{0,16},{4,20},{8,24},{12,28},{16,0},{20,4},{24,8},{28,12},{1,17},{... | collective-permute-start | bytes 516104 | tf_op jit(solution)/shard_map/ppermute | solution.py:412
  40.0 10.0 %collective-permute-start.18 = (bf16[48,1792]{1,0:T(8,128)(2,1)S(1)}, bf16[48,1792]{1,0:T(8,128)(2,1)S(1)}, u32[]{:S(2)}, u32[]{:S(2)}) collective-permute-start(bf16[48,1792]{1,0:T(8,128)(2,1)S(1)} %get-tuple-element.74.refs_0_), channel_id=1, source_target_pairs={{0,8},{4,12},{8,16},{12,20},{16,24},{20,28},{24,0},{28,4},{1,9},{5... | collective-permute-start | bytes 516104 | tf_op jit(solution)/shard_map/ppermute | solution.py:412
  50.1 16.4 %collective-permute-start.20 = (bf16[192,1792]{1,0:T(8,128)(2,1)S(1)}, bf16[192,1792]{1,0:T(8,128)(2,1)S(1)}, u32[]{:S(2)}, u32[]{:S(2)}) collective-permute-start(bf16[192,1792]{1,0:T(8,128)(2,1)S(1)} %get-tuple-element.79.refs_7_), channel_id=1, source_target_pairs={{0,4},{4,0},{8,12},{12,8},{16,20},{20,16},{24,28},{28,24},{1,5},{5... | collective-permute-start | bytes 2064392 | tf_op jit(solution)/shard_map/ppermute | solution.py:439
  50.2 8.5 %collective-permute-start.21 = (bf16[48,1792]{1,0:T(8,128)(2,1)S(1)}, bf16[48,1792]{1,0:T(8,128)(2,1)S(1)}, u32[]{:S(2)}, u32[]{:S(2)}) collective-permute-start(bf16[48,1792]{1,0:T(8,128)(2,1)S(1)} %get-tuple-element.81), channel_id=1, source_target_pairs={{0,8},{4,12},{1,9},{5,13},{2,10},{6,14},{3,11},{7,15}} | collective-permute-start | bytes 516104 | tf_op jit(solution)/shard_map/ppermute | solution.py:442
  51.6 8.5 %collective-permute-start.22 = (bf16[48,1792]{1,0:T(8,128)(2,1)S(1)}, bf16[48,1792]{1,0:T(8,128)(2,1)S(1)}, u32[]{:S(2)}, u32[]{:S(2)}) collective-permute-start(bf16[48,1792]{1,0:T(8,128)(2,1)S(1)} %get-tuple-element.82), channel_id=1, source_target_pairs={{0,16},{4,20},{1,17},{5,21},{2,18},{6,22},{3,19},{7,23}} | collective-permute-start | bytes 516104 | tf_op jit(solution)/shard_map/ppermute | solution.py:442
  53.7 8.2 %collective-permute-start.23 = (bf16[48,1792]{1,0:T(8,128)(2,1)S(1)}, bf16[48,1792]{1,0:T(8,128)(2,1)S(1)}, u32[]{:S(2)}, u32[]{:S(2)}) collective-permute-start(bf16[48,1792]{1,0:T(8,128)(2,1)S(1)} %get-tuple-element.83), channel_id=1, source_target_pairs={{0,24},{4,28},{1,25},{5,29},{2,26},{6,30},{3,27},{7,31}} | collective-permute-start | bytes 516104 | tf_op jit(solution)/shard_map/ppermute | solution.py:442
  66.5 9.6 %copy-start.2 = (s32[256]{0:T(256)S(1)}, s32[256]{0:T(256)}, u32[]{:S(2)}) copy-start(s32[256]{0:T(256)} %pivots.1) | copy-start | bytes 3076
